TPU v7x, 32 devices: a whole 2x2x4 slice. The times are simulated.
32 devices in a mesh: dp: 16 (over z, y, x), fsdp: 2 (over core).
Axes of the slice: x: 2, y: 2, z: 4, core: 2. Of those that a mesh axis runs over, the one named last changes fastest.
Arguments:
- activations: bfloat16 [8192, 8192], P('dp', 'fsdp'), may hold values from -6 to 6
- out_grads: bfloat16 [16, 896, 8192], P(None, 'fsdp', 'dp'), may hold values from -0.09375 to 0.09375
- proj_basis: bfloat16 [8192, 512], P('fsdp', 'dp'), may hold values from -0.0625 to 0.0625
- weight: bfloat16 [8192, 14336], P('fsdp', 'dp'), may hold values from -6 to 6
- ema_weight: bfloat16 [8192, 14336], P('fsdp', 'dp'), may hold values from -6 to 6
- first_moment: float32 [14336, 512], P(('dp', 'fsdp')), may hold values from -2 to 2
- second_moment: float32 [14336, 512], P(('dp', 'fsdp')), may hold values from 0.01 to 0.1
Outputs:
- new_weight: bfloat16 [8192, 14336], P('fsdp', 'dp')
- new_ema: bfloat16 [8192, 14336], P('fsdp', 'dp')
- new_first: float32 [14336, 512], P(('dp', 'fsdp'))
- new_second: float32 [14336, 512], P(('dp', 'fsdp'))
All inputs are finite; a program needn't handle non-finite values.
Results may differ from a plain program's by a relative error of at most 0.0031.
Values may be sent and summed in bfloat16 or wider, within the bound.
A program may use at most 128 MiB of HBM per device.

v0:
```python
import jax
import jax.numpy as jnp
from jax import lax
from jax.sharding import PartitionSpec as P


def on_device(activations, out_grads, proj_basis, weight, ema_weight, first_moment, second_moment):
    full_basis = lax.all_gather(proj_basis, "dp", axis=1, tiled=True)
    partial_value = jnp.dot(activations, full_basis, preferred_element_type=jnp.float32)
    projected = lax.psum(partial_value, "fsdp").astype(jnp.bfloat16)
    whole_term = jnp.einsum("ikt,tr->ikr", out_grads, projected, preferred_element_type=jnp.float32)
    local_grads = lax.psum_scatter(whole_term, "dp", scatter_dimension=0, tiled=True)
    proj_grads = local_grads.reshape(-1, local_grads.shape[-1])
    new_first = 0.9 * first_moment + 0.1 * proj_grads
    new_second = 0.95 * second_moment + 0.05 * proj_grads * proj_grads
    direction = (new_first / jnp.sqrt(new_second)).astype(jnp.bfloat16)
    update = lax.dot_general(
        full_basis,
        lax.all_gather(direction, "fsdp", axis=0, tiled=True),
        (((1,), (1,)), ((), ())),
        preferred_element_type=jnp.float32,
    )
    stepped = weight.astype(jnp.float32) - 0.2 * update
    new_ema = (0.9 * ema_weight.astype(jnp.float32) + 0.1 * stepped).astype(jnp.bfloat16)
    return (stepped.astype(jnp.bfloat16), new_ema, new_first, new_second)


def solution(mesh):
    in_specs = (
        P("dp", "fsdp"),
        P(None, "fsdp", "dp"),
        P("fsdp", "dp"),
        P("fsdp", "dp"),
        P("fsdp", "dp"),
        P(("dp", "fsdp"), None),
        P(("dp", "fsdp"), None),
    )
    out_specs = (P("fsdp", "dp"), P("fsdp", "dp"), P(("dp", "fsdp"), None), P(("dp", "fsdp"), None))
    return jax.shard_map(
        on_device, mesh=mesh, in_specs=in_specs, out_specs=out_specs, check_vma=False
    )
```

profile of v0, /device:TPU:0, one launch (start us, length us, event | category | flops | bytes accessed | tf_op | source)
XLA Modules:
  0.0 462.6 jit_solution(1593989322090599386)
XLA Ops:
  7.2 0.0 all-gather.2.cloned.1.call-start
  7.2 0.7 all-gather.2.cloned.1.call-update
  7.9 0.0 reduce-scatter.2.cloned.1.call-start
  7.9 81.6 %all-gather.2.cloned.1.call-done = bf16[4096,512]{0,1:T(8,128)(2,1)} async-done(((bf16[4096,32]{0,1:T(8,128)(2,1)}), bf16[4096,512]{0,1:T(8,128)(2,1)}) %all-gather.2.cloned.1.call-update) | async-done | bytes 4194320 | tf_op jit(solution)/shard_map/all_gather | solution.py:8
  89.6 5.8 %fusion.7 = f32[512,512]{1,0:T(8,128)S(1)} fusion(bf16[512,4096]{1,0:T(8,128)(2,1)} %param.7, bf16[4096,512]{0,1:T(8,128)(2,1)} %all-gather.2.cloned.1.call-done), kind=kOutput, calls=%fused_computation.11 | convolution fusion | flops 2147483648 | bytes 9437184 | tf_op jit(solution)/shard_map/dot_general | solution.py:9
  95.4 6.3 %all-reduce.1 = bf16[512,512]{1,0:T(8,128)(2,1)S(1)} all-reduce(f32[512,512]{1,0:T(8,128)S(1)} %fusion.7), channel_id=1, replica_groups=mesh['dp'=16,'fsdp'=2] {'fsdp'}, use_global_device_ids=true, to_apply=%region_0.0 | all-reduce | flops 262144 | bytes 1572864 | tf_op jit(solution)/shard_map/psum | solution.py:10
  101.7 10.5 %convolution_bitcast_fusion = f32[16,448,512]{2,1,0:T(8,128)} fusion(bf16[16,448,512]{2,1,0:T(8,128)(2,1)} %param.8, bf16[512,512]{1,0:T(8,128)(2,1)S(1)} %all-reduce.1), kind=kOutput, calls=%fused_computation.3 | convolution fusion | flops 3758096384 | bytes 22544384 | tf_op jit(solution)/shard_map/ikt,tr->ikr/dot_general | solution.py:11
  112.1 0.0 reduce-scatter.2.cloned.1.call-update
  112.2 10.8 %copy.11 = bf16[4096,896]{0,1:T(8,128)(2,1)} copy(bf16[4096,896]{1,0:T(8,128)(2,1)} %param.10) | data formatting | bytes 14680064 | tf_op args[3]
  123.0 0.0 copy-start
  123.0 0.0 copy-start.1
  123.0 11.0 %copy.12 = bf16[4096,896]{0,1:T(8,128)(2,1)} copy(bf16[4096,896]{1,0:T(8,128)(2,1)} %param.11) | data formatting | bytes 14680064 | tf_op args[4]
  134.0 281.1 %reduce-scatter.2.cloned.1.call-done = f32[1,448,512]{2,1,0:T(8,128)} async-done(((f32[16,448,512]{2,1,0:T(8,128)}), f32[1,448,512]{2,1,0:T(8,128)}) %reduce-scatter.2.cloned.1.call-update) | async-done | bytes 917520 | tf_op jit(solution)/shard_map/reduce_scatter | solution.py:12
  415.1 0.0 copy-done
  415.1 0.0 copy-done.1
  415.1 2.8 multiply_convert_fusion
  417.9 2.4 all_gather.7
  420.4 13.7 %add_convert_fusion = (bf16[4096,896]{0,1:T(8,128)(2,1)}, bf16[4096,896]{0,1:T(8,128)(2,1)}) fusion(bf16[4096,896]{0,1:T(8,128)(2,1)} %copy.12, bf16[4096,896]{0,1:T(8,128)(2,1)} %copy.11, bf16[896,512]{1,0:T(8,128)(2,1)S(1)} %all_gather.7, bf16[4096,512]{0,1:T(8,128)(2,1)} %all-gather.2.cloned.1.call-done), kind=kOutput, calls=%fused_computation.1 | convolution fusion | flops 3791126528 | bytes 34471936 | tf_op jit(solution)/shard_map/dot_general | solution.py:17
  434.1 10.8 %copy.13 = bf16[4096,896]{1,0:T(8,128)(2,1)} copy(bf16[4096,896]{0,1:T(8,128)(2,1)} %get-tuple-element.12) | data formatting | bytes 14680064
  444.9 10.8 %copy.14 = bf16[4096,896]{1,0:T(8,128)(2,1)} copy(bf16[4096,896]{0,1:T(8,128)(2,1)} %get-tuple-element.11) | data formatting | bytes 14680064
Async XLA Ops:
  7.2 82.4 %all-gather.2.cloned.1.call-start = ((), (), s32[]{:S(2)}) async-start(), calls=%async_computation.1 | async-start | bytes 4456448 | tf_op jit(solution)/shard_map/all_gather | solution.py:8
  7.9 407.2 %reduce-scatter.2.cloned.1.call-start = ((), (), s32[]{:S(2)}) async-start(), calls=%async_computation.2 | async-start | bytes 15597568 | tf_op jit(solution)/shard_map/reduce_scatter | solution.py:12
  123.0 292.1 %copy-start = (f32[448,512]{1,0:T(8,128)S(1)}, f32[448,512]{1,0:T(8,128)}, u32[]{:S(2)}) copy-start(f32[448,512]{1,0:T(8,128)} %param.13) | copy-start | bytes 2752516
  123.0 292.1 %copy-start.1 = (f32[448,512]{1,0:T(8,128)S(1)}, f32[448,512]{1,0:T(8,128)}, u32[]{:S(2)}) copy-start(f32[448,512]{1,0:T(8,128)} %param.12) | copy-start | bytes 2752516
Sparse Core Ops, SparseCore 0:
  10.8 78.7 all-gather.1
  112.3 302.7 reduce-scatter.1
where the time goes:
time: 468 us; the launch traced here: 463 us
  waiting for transfers between devices  363 us (78%)
  local copies, waits for them, and re-layouts  43.5 us (9%)
  matrix products  30 us (6%)
  between operations  14.1 us (3%)
  blocking collectives  8.72 us (2%)
    reduce_scatter x1, waiting for transfers between devices, on_device(): lax.psum_scatter(whole_term, 'dp', scatter_dimension=0, tiled=True)  281 us
    all_gather x1, waiting for transfers between devices, on_device(): full_basis = lax.all_gather(proj_basis, 'dp', axis=1, tiled=True)  81.6 us
    unnamed x8, local copies, waits for them, and re-layouts  43.5 us
    dot_general x1, matrix products, on_device(): lax.dot_general(full_basis, lax.all_gather(direction, 'fsdp', axis=0, til...  13.7 us
    dot_general x1, matrix products, on_device(): jnp.einsum('ikt,tr->ikr', out_grads, projected, preferred_element_type=jn...  10.5 us
  transfers between devices with their start and end apart: 2, of which 2 were waited for; matrix products, arithmetic and copies ran while one was open for 5% of the time, Pallas kernels for 0%

commit v1 on v0

v1 whole, which is shorter than its diff:
```python
import jax
import jax.numpy as jnp
from jax import lax
from jax.sharding import PartitionSpec as P

SHARES = (4, 4, 3, 3)


def pieces(whole, unit):
    if whole % unit:
        return [(0, whole)]
    count, total, ends = whole // unit, sum(SHARES), [0]
    for at in range(len(SHARES)):
        ends.append(count * sum(SHARES[: at + 1]) // total)
    return [(low * unit, high * unit) for low, high in zip(ends, ends[1:]) if high > low]


def order_of(at, bits):
    low = list(range(min(2, bits)))
    rest = list(range(len(low), bits))
    return (low if at % 2 == 0 else low[::-1]) + rest


def swap(value, bit, size):
    return lax.ppermute(value, "dp", [(i, i ^ (1 << bit)) for i in range(size)])


def gathered(block, order, size):
    me = lax.axis_index("dp")
    done, held = [], block
    for bit in order[::-1]:
        other = swap(held, bit, size)
        axis = sum(b > bit for b in done)
        mine = (me >> bit) & 1
        held = jnp.where(mine == 0, jnp.stack([held, other], axis), jnp.stack([other, held], axis))
        done.append(bit)
    return held.reshape((-1,) + block.shape[1:])


def scattered(grads, projected, order, size):
    me = lax.axis_index("dp")
    bits = len(order)
    left = list(range(bits))[::-1]

    def term(part, kind):
        out = jnp.einsum("...kt,tr->...kr", part, projected, preferred_element_type=jnp.float32)
        return out.astype(kind)

    held = grads.reshape((2,) * bits + grads.shape[1:])
    for step, bit in enumerate(order):
        axis, mine = left.index(bit), (me >> bit) & 1
        keep = lax.dynamic_index_in_dim(held, mine, axis, keepdims=False)
        give = lax.dynamic_index_in_dim(held, 1 - mine, axis, keepdims=False)
        if step == 0:
            other = swap(term(give, jnp.bfloat16), bit, size)
            keep = term(keep, jnp.float32)
        else:
            other = swap(give.astype(jnp.bfloat16), bit, size)
        held = keep + other.astype(jnp.float32)
        left.remove(bit)
    return held


def make(size):
    bits = size.bit_length() - 1

    def on_device(activations, out_grads, proj_basis, weight, ema_weight, first_moment, second_moment):
        features = proj_basis.shape[0]
        turned = proj_basis.T
        partial_value, columns = 0.0, []
        for at, (low, high) in enumerate(pieces(features, 128)):
            part = gathered(turned[:, low:high], order_of(at, bits), size)
            columns.append(part)
            partial_value += lax.dot_general(
                activations[:, low:high], part, (((1,), (1,)), ((), ())), preferred_element_type=jnp.float32
            )
        full_basis = jnp.concatenate(columns, axis=1)
        projected = lax.psum(partial_value, "fsdp").astype(jnp.bfloat16)
        proj_grads = jnp.concatenate(
            [
                scattered(out_grads[:, low:high], projected, order_of(at, bits), size)
                for at, (low, high) in enumerate(pieces(out_grads.shape[1], 16))
            ],
            axis=0,
        )
        new_first = 0.9 * first_moment + 0.1 * proj_grads
        new_second = 0.95 * second_moment + 0.05 * proj_grads * proj_grads
        direction = (new_first / jnp.sqrt(new_second)).astype(jnp.bfloat16)
        update = lax.dot_general(
            full_basis,
            lax.all_gather(direction, "fsdp", axis=0, tiled=True),
            (((0,), (1,)), ((), ())),
            preferred_element_type=jnp.float32,
        )
        stepped = weight.astype(jnp.float32) - 0.2 * update
        new_ema = (0.9 * ema_weight.astype(jnp.float32) + 0.1 * stepped).astype(jnp.bfloat16)
        return (stepped.astype(jnp.bfloat16), new_ema, new_first, new_second)

    return on_device


def solution(mesh):
    in_specs = (
        P("dp", "fsdp"),
        P(None, "fsdp", "dp"),
        P("fsdp", "dp"),
        P("fsdp", "dp"),
        P("fsdp", "dp"),
        P(("dp", "fsdp"), None),
        P(("dp", "fsdp"), None),
    )
    out_specs = (P("fsdp", "dp"), P("fsdp", "dp"), P(("dp", "fsdp"), None), P(("dp", "fsdp"), None))
    return jax.shard_map(
        make(mesh.shape["dp"]), mesh=mesh, in_specs=in_specs, out_specs=out_specs, check_vma=False
    )
```

time: 468 us -> 198 us (0.42); the launches traced: 463 us -> 198 us
  waiting for transfers between devices: 363 us -> 93 us
  starting transfers between devices: 0.08 us -> 42.5 us
  local copies, waits for them, and re-layouts: 43.5 us -> 21.3 us
  between operations: 14.1 us -> 1.42 us
  matrix products: 30 us -> 23 us
  other arithmetic: 2.77 us -> 7.45 us
    reduce_scatter x1 -> x0, waiting for transfers between devices: 281 us -> none  [on_device(): lax.psum_scatter(whole_term, 'dp', scatter_dimension=0, tiled=True)]
    ppermute x0 -> x32, waiting for transfers between devices: none -> 93 us  [swap(): return lax.ppermute(value, 'dp', [(i, i ^ 1 << bit) for i in range(size)])]
    all_gather x1 -> x0, waiting for transfers between devices: 81.6 us -> none  [on_device(): full_basis = lax.all_gather(proj_basis, 'dp', axis=1, tiled=True)]
    ppermute x0 -> x32, starting transfers between devices: none -> 42.5 us  [swap(): return lax.ppermute(value, 'dp', [(i, i ^ 1 << bit) for i in range(size)])]
    unnamed x8 -> x42, local copies, waits for them, and re-layouts: 43.5 us -> 2.81 us
    slice x0 -> x2, local copies, waits for them, and re-layouts: none -> 7.85 us  [on_device(): out_grads[:, low:high]]
    dot_general x2 -> x12, matrix products: 16.3 us -> 8.6 us  [the longest x8 5.37 us: term(): jnp.einsum('...kt,tr->...kr', part, projected, preferred_element_type=jnp...]
    squeeze x0 -> x3, local copies, waits for them, and re-layouts: none -> 6.56 us  [scattered(): keep = lax.dynamic_index_in_dim(held, mine, axis, keepdims=False)]
  transfers between devices with their start and end apart: 2 -> 32, of which waited for: 2 -> 18; matrix products, arithmetic and copies ran while one was open for 5% -> 14% of each run, Pallas kernels for 0% -> 0%
where the time goes in v1:
time: 198 us
  waiting for transfers between devices  93 us (47%)
  starting transfers between devices  42.5 us (21%)
  matrix products  23 us (12%)
  local copies, waits for them, and re-layouts  21.3 us (11%)
  blocking collectives  9.04 us (5%)
  other arithmetic  7.45 us (4%)
    ppermute x32, waiting for transfers between devices, swap(): return lax.ppermute(value, 'dp', [(i, i ^ 1 << bit) for i in range(size)])  93 us
    ppermute x32, starting transfers between devices, swap(): return lax.ppermute(value, 'dp', [(i, i ^ 1 << bit) for i in range(size)])  42.5 us
    dot_general x1, matrix products, on_device(): lax.dot_general(full_basis, lax.all_gather(direction, 'fsdp', axis=0, til...  14.4 us
    slice x2, local copies, waits for them, and re-layouts, on_device(): out_grads[:, low:high]  7.85 us
    squeeze x3, local copies, waits for them, and re-layouts, scattered(): keep = lax.dynamic_index_in_dim(held, mine, axis, keepdims=False)  6.56 us
    psum x1, blocking collectives, on_device(): projected = lax.psum(partial_value, 'fsdp').astype(jnp.bfloat16)  6.46 us
    dot_general x8, matrix products, term(): jnp.einsum('...kt,tr->...kr', part, projected, preferred_element_type=jnp...  5.37 us
  transfers between devices with their start and end apart: 32, of which 18 were waited for; matrix products, arithmetic and copies ran while one was open for 14% of the time, Pallas kernels for 0%

profile of v1, /device:TPU:0, one launch (start us, length us, event | category | flops | bytes accessed | tf_op | source)
XLA Modules:
  0.0 197.7 jit_solution(2854443087275716497)
XLA Ops:
  2.2 4.0 %collective-permute-start.12 = (bf16[32,896]{1,0:T(8,128)(2,1)}, bf16[32,896]{1,0:T(8,128)(2,1)S(1)}, u32[]{:S(2)}, u32[]{:S(2)}) collective-permute-start(bf16[32,896]{1,0:T(8,128)(2,1)} %get-tuple-element.27), channel_id=1, source_target_pairs={{0,16},{2,18},{4,20},{6,22},{8,24},{10,26},{12,28},{14,30},{16,0},... | collective-permute-start | bytes 172040 | tf_op jit(solution)/shard_map/ppermute | solution.py:25
  8.0 2.9 %collective-permute-start.4 = (bf16[32,1152]{1,0:T(8,128)(2,1)}, bf16[32,1152]{1,0:T(8,128)(2,1)S(1)}, u32[]{:S(2)}, u32[]{:S(2)}) collective-permute-start(bf16[32,1152]{1,0:T(8,128)(2,1)} %get-tuple-element.33), channel_id=1, source_target_pairs={{0,16},{2,18},{4,20},{6,22},{8,24},{10,26},{12,28},{14,30},{16,0},... | collective-permute-start | bytes 221192 | tf_op jit(solution)/shard_map/ppermute | solution.py:25
  10.9 3.9 %fusion.64 = (bf16[16,96,512]{2,1,0:T(8,128)(2,1)}, bf16[16,96,512]{2,1,0:T(8,128)(2,1)}) fusion(bf16[16,448,512]{2,1,0:T(8,128)(2,1)} %param.8), kind=kLoop, calls=%fused_computation.143 | loop fusion | bytes 6291456 | tf_op jit(solution)/shard_map/slice | solution.py:81
  14.8 3.9 %fusion.63 = (bf16[16,128,512]{2,1,0:T(8,128)(2,1)}, bf16[16,128,512]{2,1,0:T(8,128)(2,1)S(1)}) fusion(bf16[16,448,512]{2,1,0:T(8,128)(2,1)} %param.8), kind=kLoop, calls=%fused_computation.142 | loop fusion | bytes 8388608 | tf_op jit(solution)/shard_map/slice | solution.py:81
  18.7 2.6 %dynamic-slice_bitcast_fusion.3 = (bf16[2,2,2,96,512]{4,3,2,1,0:T(8,128)(2,1)}, bf16[2,2,2,96,512]{4,3,2,1,0:T(8,128)(2,1)}) fusion(bf16[2,2,2,2,96,512]{5,4,3,2,1,0:T(8,128)(2,1)} %bitcast.203, s32[]{:T(128)S(6)} %select_n.428, s32[]{:T(128)S(6)} %select_n.429), kind=kLoop, calls=%fused_computation.61 | loop fusion | bytes 3145736 | tf_op jit(solution)/shard_map/jit(dynamic_index_in_dim)/squeeze | solution.py:52
  22.6 2.7 %dynamic-slice_bitcast_fusion.5 = (bf16[2,2,2,96,512]{4,3,2,1,0:T(8,128)(2,1)}, bf16[2,2,2,96,512]{4,3,2,1,0:T(8,128)(2,1)}) fusion(bf16[2,2,2,2,96,512]{5,4,3,2,1,0:T(8,128)(2,1)} %bitcast.202, s32[]{:T(128)S(6)} %select_n.426, s32[]{:T(128)S(6)} %select_n.427), kind=kLoop, calls=%fused_computation.64 | loop fusion | bytes 3145736 | tf_op jit(solution)/shard_map/jit(dynamic_index_in_dim)/squeeze | solution.py:52
  32.8 3.9 %collective-permute-done.13 = bf16[2,32,896]{2,1,0:T(8,128)(2,1)S(1)} collective-permute-done((bf16[2,32,896]{2,1,0:T(8,128)(2,1)S(1)}, bf16[2,32,896]{2,1,0:T(8,128)(2,1)S(1)}, u32[]{:S(2)}, u32[]{:S(2)}) %collective-permute-start.13) | collective-permute-done | bytes 114720 | tf_op jit(solution)/shard_map/ppermute | solution.py:25
  48.6 4.3 %collective-permute-done.2 = bf16[2,2,32,1152]{3,2,1,0:T(8,128)(2,1)S(1)} collective-permute-done((bf16[2,2,32,1152]{3,2,1,0:T(8,128)(2,1)S(1)}, bf16[2,2,32,1152]{3,2,1,0:T(8,128)(2,1)S(1)}, u32[]{:S(2)}, u32[]{:S(2)}) %collective-permute-start.2) | collective-permute-done | bytes 294944 | tf_op jit(solution)/shard_map/ppermute | solution.py:25
  55.7 5.4 %collective-permute-done.11 = bf16[2,2,2,32,896]{4,3,0,1,2:T(8,128)(2,1)S(1)} collective-permute-done((bf16[2,2,2,32,896]{4,3,0,1,2:T(8,128)(2,1)S(1)}, bf16[2,2,2,32,896]{4,3,0,1,2:T(8,128)(2,1)S(1)}, u32[]{:S(2)}, u32[]{:S(2)}) %collective-permute-start.11) | collective-permute-done | bytes 458784 | tf_op jit(solution)/shard_map/ppermute | solution.py:25
  63.0 10.5 %collective-permute-done.7 = bf16[2,2,2,32,1152]{4,3,0,1,2:T(8,128)(2,1)S(1)} collective-permute-done((bf16[2,2,2,32,1152]{4,3,0,1,2:T(8,128)(2,1)S(1)}, bf16[2,2,2,32,1152]{4,3,0,1,2:T(8,128)(2,1)S(1)}, u32[]{:S(2)}, u32[]{:S(2)}) %collective-permute-start.7) | collective-permute-done | bytes 589856 | tf_op jit(solution)/shard_map/ppermute | solution.py:25
  74.1 2.7 %copy-done.13 = bf16[512,4096]{1,0:T(8,128)(2,1)S(1)} copy-done((bf16[512,4096]{1,0:T(8,128)(2,1)S(1)}, bf16[512,4096]{1,0:T(8,128)(2,1)}, u32[]{:S(2)}) %copy-start.13) | copy-done | bytes 4194328
  80.1 6.5 %all-reduce.1 = bf16[512,512]{0,1:T(8,128)(2,1)S(1)} all-reduce(f32[512,512]{0,1:T(8,128)S(1)} %fusion.9), channel_id=1, replica_groups=mesh['dp'=16,'fsdp'=2] {'fsdp'}, use_global_device_ids=true, to_apply=%region_0.1 | all-reduce | flops 262144 | bytes 1572864 | tf_op jit(solution)/shard_map/psum | solution.py:78
  93.6 14.0 %collective-permute-done.28 = bf16[2,2,2,96,512]{4,3,0,1,2:T(8,128)(2,1)S(1)} collective-permute-done((bf16[2,2,2,96,512]{4,3,0,1,2:T(8,128)(2,1)S(1)}, bf16[2,2,2,96,512]{4,3,0,1,2:T(8,128)(2,1)S(1)}, u32[]{:S(2)}, u32[]{:S(2)}) %collective-permute-start.28) | collective-permute-done | bytes 786464 | tf_op jit(solution)/shard_map/ppermute | solution.py:25
  111.2 21.2 %collective-permute-done.16 = bf16[2,2,2,128,512]{4,3,2,1,0:T(8,128)(2,1)S(1)} collective-permute-done((bf16[2,2,2,128,512]{4,3,2,1,0:T(8,128)(2,1)S(1)}, bf16[2,2,2,128,512]{4,3,2,1,0:T(8,128)(2,1)S(1)}, u32[]{:S(2)}, u32[]{:S(2)}) %collective-permute-start.16) | collective-permute-done | bytes 1048608 | tf_op jit(solution)/shard_map/ppermute | solution.py:25
  135.1 5.7 %collective-permute-done.29 = bf16[2,2,96,512]{3,2,0,1:T(8,128)(2,1)S(1)} collective-permute-done((bf16[2,2,96,512]{3,2,0,1:T(8,128)(2,1)S(1)}, bf16[2,2,96,512]{3,2,0,1:T(8,128)(2,1)S(1)}, u32[]{:S(2)}, u32[]{:S(2)}) %collective-permute-start.29) | collective-permute-done | bytes 393248 | tf_op jit(solution)/shard_map/ppermute | solution.py:25
  143.3 6.1 %collective-permute-done.30 = bf16[2,96,512]{2,1,0:T(8,128)(2,1)S(1)} collective-permute-done((bf16[2,96,512]{2,1,0:T(8,128)(2,1)S(1)}, bf16[2,96,512]{2,1,0:T(8,128)(2,1)S(1)}, u32[]{:S(2)}, u32[]{:S(2)}) %collective-permute-start.30) | collective-permute-done | bytes 196640 | tf_op jit(solution)/shard_map/ppermute | solution.py:25
  149.4 2.1 %collective-permute-start.31 = (bf16[96,512]{1,0:T(8,128)(2,1)S(1)}, bf16[96,512]{1,0:T(8,128)(2,1)S(1)}, u32[]{:S(2)}, u32[]{:S(2)}) collective-permute-start(bf16[96,512]{1,0:T(8,128)(2,1)S(1)} %fusion.58), channel_id=1, source_target_pairs={{0,16},{2,18},{4,20},{6,22},{8,24},{10,26},{12,28},{14,30},{16,0},... | collective-permute-start | bytes 294920 | tf_op jit(solution)/shard_map/ppermute | solution.py:25
  151.7 3.3 %collective-permute-start.27 = (bf16[96,512]{1,0:T(8,128)(2,1)S(1)}, bf16[96,512]{1,0:T(8,128)(2,1)S(1)}, u32[]{:S(2)}, u32[]{:S(2)}) collective-permute-start(bf16[96,512]{1,0:T(8,128)(2,1)S(1)} %fusion.57), channel_id=1, source_target_pairs={{0,16},{2,18},{4,20},{6,22},{8,24},{10,26},{12,28},{14,30},{16,0},... | collective-permute-start | bytes 294920 | tf_op jit(solution)/shard_map/ppermute | solution.py:25
  156.5 2.2 %collective-permute-done.27 = bf16[96,512]{1,0:T(8,128)(2,1)S(1)} collective-permute-done((bf16[96,512]{1,0:T(8,128)(2,1)S(1)}, bf16[96,512]{1,0:T(8,128)(2,1)S(1)}, u32[]{:S(2)}, u32[]{:S(2)}) %collective-permute-start.27) | collective-permute-done | bytes 98336 | tf_op jit(solution)/shard_map/ppermute | solution.py:25
  161.4 6.0 %collective-permute-done.18 = bf16[2,128,512]{2,1,0:T(8,128)(2,1)S(1)} collective-permute-done((bf16[2,128,512]{2,1,0:T(8,128)(2,1)S(1)}, bf16[2,128,512]{2,1,0:T(8,128)(2,1)S(1)}, u32[]{:S(2)}, u32[]{:S(2)}) %collective-permute-start.18) | collective-permute-done | bytes 262176 | tf_op jit(solution)/shard_map/ppermute | solution.py:25
  167.5 2.3 %collective-permute-start.19 = (bf16[128,512]{1,0:T(8,128)(2,1)S(1)}, bf16[128,512]{1,0:T(8,128)(2,1)S(1)}, u32[]{:S(2)}, u32[]{:S(2)}) collective-permute-start(bf16[128,512]{1,0:T(8,128)(2,1)S(1)} %fusion.54), channel_id=1, source_target_pairs={{0,16},{2,18},{4,20},{6,22},{8,24},{10,26},{12,28},{14,30},{16,0},... | collective-permute-start | bytes 393224 | tf_op jit(solution)/shard_map/ppermute | solution.py:25
  175.6 3.4 %collective-permute-done.23 = bf16[128,512]{1,0:T(8,128)(2,1)S(1)} collective-permute-done((bf16[128,512]{1,0:T(8,128)(2,1)S(1)}, bf16[128,512]{1,0:T(8,128)(2,1)S(1)}, u32[]{:S(2)}, u32[]{:S(2)}) %collective-permute-start.23) | collective-permute-done | bytes 131104 | tf_op jit(solution)/shard_map/ppermute | solution.py:25
  180.7 2.6 %all_gather.3 = bf16[896,512]{1,0:T(8,128)(2,1)} all-gather(bf16[448,512]{1,0:T(8,128)(2,1)S(1)} %get-tuple-element.4), channel_id=1, replica_groups=mesh['dp'=16,'fsdp'=2] {'fsdp'}, dimensions={0}, use_global_device_ids=true | all-gather | bytes 1376256 | tf_op jit(solution)/shard_map/all_gather | solution.py:91
  183.3 14.4 %add_convert_fusion = (bf16[4096,896]{1,0:T(8,128)(2,1)}, bf16[4096,896]{1,0:T(8,128)(2,1)}) fusion(bf16[4096,896]{1,0:T(8,128)(2,1)} %param.11, bf16[4096,896]{1,0:T(8,128)(2,1)} %param.10, bf16[896,512]{1,0:T(8,128)(2,1)} %all_gather.3, bf16[512,896]{1,0:T(8,128)(2,1)S(1)} %bitcast.209, bf16[512,896]{1,0:T(8,128)(2,1)S(1)} %bitcast.207, ...), kind=kOutput, calls=%fused_computation | convolution fusion | flops 3807903744 | bytes 34471936 | tf_op jit(solution)/shard_map/dot_general | solution.py:89
  (169 shorter events, 59.7 us)
Async XLA Ops:
  2.2 27.8 %collective-permute-start.12 = (bf16[32,896]{1,0:T(8,128)(2,1)}, bf16[32,896]{1,0:T(8,128)(2,1)S(1)}, u32[]{:S(2)}, u32[]{:S(2)}) collective-permute-start(bf16[32,896]{1,0:T(8,128)(2,1)} %get-tuple-element.27), channel_id=1, source_target_pairs={{0,16},{2,18},{4,20},{6,22},{8,24},{10,26},{12,28},{14,30},{16,0},... | collective-permute-start | bytes 172040 | tf_op jit(solution)/shard_map/ppermute | solution.py:25
  6.3 19.1 %collective-permute-start.8 = (bf16[32,896]{1,0:T(8,128)(2,1)}, bf16[32,896]{1,0:T(8,128)(2,1)}, u32[]{:S(2)}, u32[]{:S(2)}) collective-permute-start(bf16[32,896]{1,0:T(8,128)(2,1)} %get-tuple-element.28), channel_id=1, source_target_pairs={{0,16},{2,18},{4,20},{6,22},{8,24},{10,26},{12,28},{14,30},{16,0},... | collective-permute-start | bytes 172040 | tf_op jit(solution)/shard_map/ppermute | solution.py:25
  8.0 22.4 %collective-permute-start.4 = (bf16[32,1152]{1,0:T(8,128)(2,1)}, bf16[32,1152]{1,0:T(8,128)(2,1)S(1)}, u32[]{:S(2)}, u32[]{:S(2)}) collective-permute-start(bf16[32,1152]{1,0:T(8,128)(2,1)} %get-tuple-element.33), channel_id=1, source_target_pairs={{0,16},{2,18},{4,20},{6,22},{8,24},{10,26},{12,28},{14,30},{16,0},... | collective-permute-start | bytes 221192 | tf_op jit(solution)/shard_map/ppermute | solution.py:25
  10.8 19.6 %collective-permute-start = (bf16[32,1152]{1,0:T(8,128)(2,1)}, bf16[32,1152]{1,0:T(8,128)(2,1)S(1)}, u32[]{:S(2)}, u32[]{:S(2)}) collective-permute-start(bf16[32,1152]{1,0:T(8,128)(2,1)} %get-tuple-element.34), channel_id=1, source_target_pairs={{0,16},{2,18},{4,20},{6,22},{8,24},{10,26},{12,28},{14,30},{16,0},... | collective-permute-start | bytes 221192 | tf_op jit(solution)/shard_map/ppermute | solution.py:25
  28.1 10.5 %collective-permute-start.9 = (bf16[2,32,896]{2,1,0:T(8,128)(2,1)S(1)}, bf16[2,32,896]{2,1,0:T(8,128)(2,1)S(1)}, u32[]{:S(2)}, u32[]{:S(2)}) collective-permute-start(bf16[2,32,896]{2,1,0:T(8,128)(2,1)S(1)} %maximum_select_fusion.21), channel_id=1, source_target_pairs={{0,8},{2,10},{4,12},{6,14},{8,0},{10,2},{12,4},{14,6},{16,24},{18,... | collective-permute-start | bytes 344072 | tf_op jit(solution)/shard_map/ppermute | solution.py:25
  30.6 12.3 %collective-permute-start.1 = (bf16[2,32,1152]{2,1,0:T(8,128)(2,1)S(1)}, bf16[2,32,1152]{2,1,0:T(8,128)(2,1)S(1)}, u32[]{:S(2)}, u32[]{:S(2)}) collective-permute-start(bf16[2,32,1152]{2,1,0:T(8,128)(2,1)S(1)} %maximum_select_fusion.18), channel_id=1, source_target_pairs={{0,8},{2,10},{4,12},{6,14},{8,0},{10,2},{12,4},{14,6},{16,24},{18,... | collective-permute-start | bytes 442376 | tf_op jit(solution)/shard_map/ppermute | solution.py:25
  32.5 8.7 %collective-permute-start.5 = (bf16[2,32,1152]{2,1,0:T(8,128)(2,1)S(1)}, bf16[2,32,1152]{2,1,0:T(8,128)(2,1)S(1)}, u32[]{:S(2)}, u32[]{:S(2)}) collective-permute-start(bf16[2,32,1152]{2,1,0:T(8,128)(2,1)S(1)} %maximum_select_fusion.20), channel_id=1, source_target_pairs={{0,8},{2,10},{4,12},{6,14},{8,0},{10,2},{12,4},{14,6},{16,24},{18,... | collective-permute-start | bytes 442376 | tf_op jit(solution)/shard_map/ppermute | solution.py:25
  36.7 9.6 %collective-permute-start.14 = (bf16[2,2,32,896]{3,2,0,1:T(8,128)(2,1)S(1)}, bf16[2,2,32,896]{3,2,0,1:T(8,128)(2,1)S(1)}, u32[]{:S(2)}, u32[]{:S(2)}) collective-permute-start(bf16[2,2,32,896]{3,2,0,1:T(8,128)(2,1)S(1)} %maximum_select_fusion.17), channel_id=1, source_target_pairs={{0,2},{2,0},{4,6},{6,4},{8,10},{10,8},{12,14},{14,12},{16,18},{18,... | collective-permute-start | bytes 688136 | tf_op jit(solution)/shard_map/ppermute | solution.py:25
  41.2 12.4 %collective-permute-start.6 = (bf16[2,2,32,1152]{3,2,0,1:T(8,128)(2,1)S(1)}, bf16[2,2,32,1152]{3,2,0,1:T(8,128)(2,1)S(1)}, u32[]{:S(2)}, u32[]{:S(2)}) collective-permute-start(bf16[2,2,32,1152]{3,2,0,1:T(8,128)(2,1)S(1)} %maximum_select_fusion.13), channel_id=1, source_target_pairs={{0,2},{2,0},{4,6},{6,4},{8,10},{10,8},{12,14},{14,12},{16,18},{18,... | collective-permute-start | bytes 884744 | tf_op jit(solution)/shard_map/ppermute | solution.py:25
  42.9 10.0 %collective-permute-start.2 = (bf16[2,2,32,1152]{3,2,1,0:T(8,128)(2,1)S(1)}, bf16[2,2,32,1152]{3,2,1,0:T(8,128)(2,1)S(1)}, u32[]{:S(2)}, u32[]{:S(2)}) collective-permute-start(bf16[2,2,32,1152]{3,2,1,0:T(8,128)(2,1)S(1)} %maximum_select_fusion.11), channel_id=1, source_target_pairs={{0,4},{2,6},{4,0},{6,2},{8,12},{10,14},{12,8},{14,10},{16,20},{18,... | collective-permute-start | bytes 884744 | tf_op jit(solution)/shard_map/ppermute | solution.py:25
  46.2 14.9 %collective-permute-start.11 = (bf16[2,2,2,32,896]{4,3,0,1,2:T(8,128)(2,1)S(1)}, bf16[2,2,2,32,896]{4,3,0,1,2:T(8,128)(2,1)S(1)}, u32[]{:S(2)}, u32[]{:S(2)}) collective-permute-start(bf16[2,2,2,32,896]{4,3,0,1,2:T(8,128)(2,1)S(1)} %maximum_select_fusion.8), channel_id=1, source_target_pairs={{0,2},{2,0},{4,6},{6,4},{8,10},{10,8},{12,14},{14,12},{16,18},{18,... | collective-permute-start | bytes 1376264 | tf_op jit(solution)/shard_map/ppermute | solution.py:25
  46.4 16.4 %collective-permute-start.15 = (bf16[2,2,2,32,896]{4,3,0,1,2:T(8,128)(2,1)S(1)}, bf16[2,2,2,32,896]{4,3,0,1,2:T(8,128)(2,1)S(1)}, u32[]{:S(2)}, u32[]{:S(2)}) collective-permute-start(bf16[2,2,2,32,896]{4,3,0,1,2:T(8,128)(2,1)S(1)} %maximum_select_fusion.10), channel_id=1, source_target_pairs={{0,4},{2,6},{4,0},{6,2},{8,12},{10,14},{12,8},{14,10},{16,20},{18,... | collective-permute-start | bytes 1376264 | tf_op jit(solution)/shard_map/ppermute | solution.py:25
  53.0 20.9 %collective-permute-start.3 = (bf16[2,2,2,32,1152]{4,3,2,1,0:T(8,128)(2,1)S(1)}, bf16[2,2,2,32,1152]{4,3,2,1,0:T(8,128)(2,1)S(1)}, u32[]{:S(2)}, u32[]{:S(2)}) collective-permute-start(bf16[2,2,2,32,1152]{4,3,2,1,0:T(8,128)(2,1)S(1)} %maximum_select_fusion.4), channel_id=1, source_target_pairs={{0,2},{2,0},{4,6},{6,4},{8,10},{10,8},{12,14},{14,12},{16,18},{18,... | collective-permute-start | bytes 1769480 | tf_op jit(solution)/shard_map/ppermute | solution.py:25
  53.7 19.8 %collective-permute-start.7 = (bf16[2,2,2,32,1152]{4,3,0,1,2:T(8,128)(2,1)S(1)}, bf16[2,2,2,32,1152]{4,3,0,1,2:T(8,128)(2,1)S(1)}, u32[]{:S(2)}, u32[]{:S(2)}) collective-permute-start(bf16[2,2,2,32,1152]{4,3,0,1,2:T(8,128)(2,1)S(1)} %maximum_select_fusion.6), channel_id=1, source_target_pairs={{0,4},{2,6},{4,0},{6,2},{8,12},{10,14},{12,8},{14,10},{16,20},{18,... | collective-permute-start | bytes 1769480 | tf_op jit(solution)/shard_map/ppermute | solution.py:25
  87.2 20.4 %collective-permute-start.28 = (bf16[2,2,2,96,512]{4,3,0,1,2:T(8,128)(2,1)S(1)}, bf16[2,2,2,96,512]{4,3,0,1,2:T(8,128)(2,1)S(1)}, u32[]{:S(2)}, u32[]{:S(2)}) collective-permute-start(bf16[2,2,2,96,512]{4,3,0,1,2:T(8,128)(2,1)S(1)} %convolution_convert_fusion.2), channel_id=1, source_target_pairs={{0,4},{2,6},{4,0},{6,2},{8,12},{10,14},{12,8},{14,10},{16,20},{18,... | collective-permute-start | bytes 2359304 | tf_op jit(solution)/shard_map/ppermute | solution.py:25
  89.4 20.5 %collective-permute-start.24 = (bf16[2,2,2,96,512]{4,3,0,1,2:T(8,128)(2,1)S(1)}, bf16[2,2,2,96,512]{4,3,0,1,2:T(8,128)(2,1)S(1)}, u32[]{:S(2)}, u32[]{:S(2)}) collective-permute-start(bf16[2,2,2,96,512]{4,3,0,1,2:T(8,128)(2,1)S(1)} %convolution_convert_fusion.3), channel_id=1, source_target_pairs={{0,2},{2,0},{4,6},{6,4},{8,10},{10,8},{12,14},{14,12},{16,18},{18,... | collective-permute-start | bytes 2359304 | tf_op jit(solution)/shard_map/ppermute | solution.py:25
  90.8 41.6 %collective-permute-start.16 = (bf16[2,2,2,128,512]{4,3,2,1,0:T(8,128)(2,1)S(1)}, bf16[2,2,2,128,512]{4,3,2,1,0:T(8,128)(2,1)S(1)}, u32[]{:S(2)}, u32[]{:S(2)}) collective-permute-start(bf16[2,2,2,128,512]{4,3,2,1,0:T(8,128)(2,1)S(1)} %convolution_convert_fusion.1), channel_id=1, source_target_pairs={{0,2},{2,0},{4,6},{6,4},{8,10},{10,8},{12,14},{14,12},{16,18},{18,... | collective-permute-start | bytes 3145736 | tf_op jit(solution)/shard_map/ppermute | solution.py:25
  93.1 40.6 %collective-permute-start.20 = (bf16[2,2,2,128,512]{4,3,0,1,2:T(8,128)(2,1)S(1)}, bf16[2,2,2,128,512]{4,3,0,1,2:T(8,128)(2,1)S(1)}, u32[]{:S(2)}, u32[]{:S(2)}) collective-permute-start(bf16[2,2,2,128,512]{4,3,0,1,2:T(8,128)(2,1)S(1)} %convolution_convert_fusion), channel_id=1, source_target_pairs={{0,4},{2,6},{4,0},{6,2},{8,12},{10,14},{12,8},{14,10},{16,20},{18,... | collective-permute-start | bytes 3145736 | tf_op jit(solution)/shard_map/ppermute | solution.py:25
  108.3 32.5 %collective-permute-start.29 = (bf16[2,2,96,512]{3,2,0,1:T(8,128)(2,1)S(1)}, bf16[2,2,96,512]{3,2,0,1:T(8,128)(2,1)S(1)}, u32[]{:S(2)}, u32[]{:S(2)}) collective-permute-start(bf16[2,2,96,512]{3,2,0,1:T(8,128)(2,1)S(1)} %fusion.49), channel_id=1, source_target_pairs={{0,2},{2,0},{4,6},{6,4},{8,10},{10,8},{12,14},{14,12},{16,18},{18,... | collective-permute-start | bytes 1179656 | tf_op jit(solution)/shard_map/ppermute | solution.py:25
  110.5 32.1 %collective-permute-start.25 = (bf16[2,2,96,512]{3,2,0,1:T(8,128)(2,1)S(1)}, bf16[2,2,96,512]{3,2,0,1:T(8,128)(2,1)S(1)}, u32[]{:S(2)}, u32[]{:S(2)}) collective-permute-start(bf16[2,2,96,512]{3,2,0,1:T(8,128)(2,1)S(1)} %fusion.48), channel_id=1, source_target_pairs={{0,4},{2,6},{4,0},{6,2},{8,12},{10,14},{12,8},{14,10},{16,20},{18,... | collective-permute-start | bytes 1179656 | tf_op jit(solution)/shard_map/ppermute | solution.py:25
  133.2 25.6 %collective-permute-start.17 = (bf16[2,2,128,512]{3,2,1,0:T(8,128)(2,1)S(1)}, bf16[2,2,128,512]{3,2,1,0:T(8,128)(2,1)S(1)}, u32[]{:S(2)}, u32[]{:S(2)}) collective-permute-start(bf16[2,2,128,512]{3,2,1,0:T(8,128)(2,1)S(1)} %fusion.38), channel_id=1, source_target_pairs={{0,4},{2,6},{4,0},{6,2},{8,12},{10,14},{12,8},{14,10},{16,20},{18,... | collective-permute-start | bytes 1572872 | tf_op jit(solution)/shard_map/ppermute | solution.py:25
  134.6 24.7 %collective-permute-start.21 = (bf16[2,2,128,512]{3,2,0,1:T(8,128)(2,1)S(1)}, bf16[2,2,128,512]{3,2,0,1:T(8,128)(2,1)S(1)}, u32[]{:S(2)}, u32[]{:S(2)}) collective-permute-start(bf16[2,2,128,512]{3,2,0,1:T(8,128)(2,1)S(1)} %fusion.39), channel_id=1, source_target_pairs={{0,2},{2,0},{4,6},{6,4},{8,10},{10,8},{12,14},{14,12},{16,18},{18,... | collective-permute-start | bytes 1572872 | tf_op jit(solution)/shard_map/ppermute | solution.py:25
  142.8 8.8 %collective-permute-start.26 = (bf16[2,96,512]{2,1,0:T(8,128)(2,1)S(1)}, bf16[2,96,512]{2,1,0:T(8,128)(2,1)S(1)}, u32[]{:S(2)}, u32[]{:S(2)}) collective-permute-start(bf16[2,96,512]{2,1,0:T(8,128)(2,1)S(1)} %fusion.52), channel_id=1, source_target_pairs={{0,8},{2,10},{4,12},{6,14},{8,0},{10,2},{12,4},{14,6},{16,24},{18,... | collective-permute-start | bytes 589832 | tf_op jit(solution)/shard_map/ppermute | solution.py:25
  159.5 12.1 %collective-permute-start.22 = (bf16[2,128,512]{2,1,0:T(8,128)(2,1)S(1)}, bf16[2,128,512]{2,1,0:T(8,128)(2,1)S(1)}, u32[]{:S(2)}, u32[]{:S(2)}) collective-permute-start(bf16[2,128,512]{2,1,0:T(8,128)(2,1)S(1)} %fusion.51), channel_id=1, source_target_pairs={{0,8},{2,10},{4,12},{6,14},{8,0},{10,2},{12,4},{14,6},{16,24},{18,... | collective-permute-start | bytes 786440 | tf_op jit(solution)/shard_map/ppermute | solution.py:25
  (29 other events, 219.0 us)

commit v2 on v0

v2 whole, which is shorter than its diff:
```python
import jax
import jax.numpy as jnp
from jax import lax
from jax.sharding import PartitionSpec as P

SHARES = (1, 1, 1)
ORDERS = ((0, 2, 1), (1, 0, 2), (2, 1, 0))


def pieces(whole, unit):
    if whole % unit or whole // unit < len(SHARES):
        return [(0, whole)]
    count, total, ends = whole // unit, sum(SHARES), [0]
    for at in range(len(SHARES)):
        ends.append(count * sum(SHARES[: at + 1]) // total)
    return [(low * unit, high * unit) for low, high in zip(ends, ends[1:]) if high > low]


def swap(value, bit, size):
    return lax.ppermute(value, "dp", [(i, i ^ (1 << bit)) for i in range(size)])


def bit_of(bit):
    return (lax.axis_index("dp") >> bit) & 1


def grown(held, bit, done, size):
    other, mine = swap(held, bit, size), bit_of(bit)
    axis = sum(b > bit for b in done)
    done.append(bit)
    return jnp.where(mine == 0, jnp.stack([held, other], axis), jnp.stack([other, held], axis))


def turns(bits):
    own = min(3, bits)
    return [[bit for bit in order if bit < own] for order in ORDERS], list(range(own, bits))


def gathered(block, bits, size, grads):
    orders, shared = turns(bits)
    cuts = pieces(block.shape[1], 128)
    held, first = block, []
    for bit in shared[::-1]:
        held = grown(held, bit, first, size)
    parts = []
    for at, (start, end) in enumerate(cuts):
        part, done = held[..., start:end], list(first)
        for turn, bit in enumerate(orders[at][::-1]):
            if at == 0 and turn == len(orders[at]) - 1:
                part, grads = lax.optimization_barrier((part, grads))
            part = grown(part, bit, done, size)
        parts.append(part.reshape(-1, end - start))
    return cuts, parts, grads


def shrunk(held, bit, left, size):
    axis, mine = left.index(bit), bit_of(bit)
    left.remove(bit)
    keep = lax.dynamic_index_in_dim(held, mine, axis, keepdims=False)
    give = lax.dynamic_index_in_dim(held, 1 - mine, axis, keepdims=False)
    return keep + swap(give.astype(jnp.bfloat16), bit, size).astype(jnp.float32)


def started(grads, projected, bit, left, size):
    axis, mine = left.index(bit), bit_of(bit)
    left.remove(bit)

    def term(which, kind):
        part = lax.dynamic_index_in_dim(grads, which, axis, keepdims=False)
        out = jnp.einsum("...kt,tr->...kr", part, projected, preferred_element_type=jnp.float32)
        return out.astype(kind)

    other = swap(term(1 - mine, jnp.bfloat16), bit, size)
    return term(mine, jnp.float32) + other.astype(jnp.float32)


def scattered(grads, projected, bits, size):
    orders, shared = turns(bits)
    sums = []
    for at, (start, end) in enumerate(pieces(grads.shape[1], 16)):
        part = grads[:, start:end].reshape((2,) * bits + (end - start, grads.shape[2]))
        left = list(range(bits))[::-1]
        held = started(part, projected, orders[at][0], left, size)
        for bit in orders[at][1:]:
            held = shrunk(held, bit, left, size)
        sums.append(held)
    total = jnp.concatenate(sums, axis=-2)
    for bit in shared:
        total = shrunk(total, bit, left, size)
    return total


def summed(value, devices):
    if devices == 2:
        return value + lax.ppermute(value, "fsdp", [(0, 1), (1, 0)])
    return lax.psum(value, "fsdp")


def make(size, devices):
    bits = size.bit_length() - 1

    def on_device(activations, out_grads, proj_basis, weight, ema_weight, first_moment, second_moment):
        cuts, columns, out_grads = gathered(proj_basis.T, bits, size, out_grads)
        partial_value = 0.0
        for (low, high), part in zip(cuts, columns):
            partial_value += lax.dot_general(
                activations[:, low:high], part, (((1,), (1,)), ((), ())), preferred_element_type=jnp.float32
            )
        full_basis = jnp.concatenate(columns, axis=1)
        projected = summed(partial_value, devices).astype(jnp.bfloat16)
        proj_grads = scattered(out_grads, projected, bits, size)
        new_first = 0.9 * first_moment + 0.1 * proj_grads
        new_second = 0.95 * second_moment + 0.05 * proj_grads * proj_grads
        direction = (new_first / jnp.sqrt(new_second)).astype(jnp.bfloat16)
        update = lax.dot_general(
            full_basis,
            lax.all_gather(direction, "fsdp", axis=0, tiled=True),
            (((0,), (1,)), ((), ())),
            preferred_element_type=jnp.float32,
        )
        stepped = weight.astype(jnp.float32) - 0.2 * update
        new_ema = (0.9 * ema_weight.astype(jnp.float32) + 0.1 * stepped).astype(jnp.bfloat16)
        return (stepped.astype(jnp.bfloat16), new_ema, new_first, new_second)

    return on_device


def solution(mesh):
    in_specs = (
        P("dp", "fsdp"),
        P(None, "fsdp", "dp"),
        P("fsdp", "dp"),
        P("fsdp", "dp"),
        P("fsdp", "dp"),
        P(("dp", "fsdp"), None),
        P(("dp", "fsdp"), None),
    )
    out_specs = (P("fsdp", "dp"), P("fsdp", "dp"), P(("dp", "fsdp"), None), P(("dp", "fsdp"), None))
    return jax.shard_map(
        make(mesh.shape["dp"], mesh.shape["fsdp"]), mesh=mesh, in_specs=in_specs, out_specs=out_specs, check_vma=False
    )
```

time: 468 us -> 170 us (0.36); the launches traced: 463 us -> 170 us
  waiting for transfers between devices: 363 us -> 89.6 us
  local copies, waits for them, and re-layouts: 43.5 us -> 7.05 us
  starting transfers between devices: 0.08 us -> 29 us
  between operations: 14.1 us -> 1.02 us
  other arithmetic: 2.77 us -> 10.4 us
  blocking collectives: 8.72 us -> 2.45 us
    reduce_scatter x1 -> x0, waiting for transfers between devices: 281 us -> none  [on_device(): lax.psum_scatter(whole_term, 'dp', scatter_dimension=0, tiled=True)]
    ppermute x0 -> x21, waiting for transfers between devices: none -> 89.6 us  [the longest x20 89.4 us: swap(): return lax.ppermute(value, 'dp', [(i, i ^ 1 << bit) for i in range(size)])]
    all_gather x1 -> x0, waiting for transfers between devices: 81.6 us -> none  [on_device(): full_basis = lax.all_gather(proj_basis, 'dp', axis=1, tiled=True)]
    unnamed x8 -> x16, local copies, waits for them, and re-layouts: 43.5 us -> 0.61 us
    ppermute x0 -> x21, starting transfers between devices: none -> 29 us  [the longest x20 29 us: swap(): return lax.ppermute(value, 'dp', [(i, i ^ 1 << bit) for i in range(size)])]
    psum x1 -> x0, blocking collectives: 6.27 us -> none  [on_device(): projected = lax.psum(partial_value, 'fsdp').astype(jnp.bfloat16)]
    slice x0 -> x2, local copies, waits for them, and re-layouts: none -> 4.74 us  [scattered(): grads[:, start:end].reshape((2,) * bits + (end - start, grads.shape[2]))]
    dot_general x2 -> x9, matrix products: 16.3 us -> 16.6 us  [the longest x6 12.6 us: term(): jnp.einsum('...kt,tr->...kr', part, projected, preferred_element_type=jnp...]
  transfers between devices with their start and end apart: 2 -> 21, of which waited for: 2 -> 16; matrix products, arithmetic and copies ran while one was open for 5% -> 11% of each run, Pallas kernels for 0% -> 0%
where the time goes in v2:
time: 170 us
  waiting for transfers between devices  89.6 us (53%)
  matrix products  30.4 us (18%)
  starting transfers between devices  29 us (17%)
  other arithmetic  10.4 us (6%)
  local copies, waits for them, and re-layouts  7.05 us (4%)
  blocking collectives  2.45 us (1%)
    ppermute x20, waiting for transfers between devices, swap(): return lax.ppermute(value, 'dp', [(i, i ^ 1 << bit) for i in range(size)])  89.4 us
    ppermute x20, starting transfers between devices, swap(): return lax.ppermute(value, 'dp', [(i, i ^ 1 << bit) for i in range(size)])  29 us
    dot_general x1, matrix products, on_device(): lax.dot_general(full_basis, lax.all_gather(direction, 'fsdp', axis=0, til...  13.9 us
    dot_general x6, matrix products, term(): jnp.einsum('...kt,tr->...kr', part, projected, preferred_element_type=jnp...  12.6 us
    slice x2, local copies, waits for them, and re-layouts, scattered(): grads[:, start:end].reshape((2,) * bits + (end - start, grads.shape[2]))  4.74 us
    dot_general x3, matrix products, on_device(): lax.dot_general(activations[:, low:high], part, (((1,), (1,)), ((), ())),...  3.96 us
  transfers between devices with their start and end apart: 21, of which 16 were waited for; matrix products, arithmetic and copies ran while one was open for 11% of the time, Pallas kernels for 0%

profile of v2, /device:TPU:0, one launch (start us, length us, event | category | flops | bytes accessed | tf_op | source)
XLA Modules:
  0.0 170.0 jit_solution(4164156682535971523)
XLA Ops:
  0.6 4.1 %collective-permute-start = (bf16[32,4096]{1,0:T(8,128)(2,1)}, bf16[32,4096]{1,0:T(8,128)(2,1)S(1)}, u32[]{:S(2)}, u32[]{:S(2)}) collective-permute-start(bf16[32,4096]{1,0:T(8,128)(2,1)} %bitcast.153), channel_id=1, source_target_pairs={{0,16},{2,18},{4,20},{6,22},{8,24},{10,26},{12,28},{14,30},{16,0},... | collective-permute-start | bytes 786440 | tf_op jit(solution)/shard_map/ppermute | solution.py:20
  4.7 12.1 %collective-permute-done = bf16[32,4096]{1,0:T(8,128)(2,1)S(1)} collective-permute-done((bf16[32,4096]{1,0:T(8,128)(2,1)}, bf16[32,4096]{1,0:T(8,128)(2,1)S(1)}, u32[]{:S(2)}, u32[]{:S(2)}) %collective-permute-start) | collective-permute-done | bytes 262176 | tf_op jit(solution)/shard_map/ppermute | solution.py:20
  25.3 3.2 %collective-permute-done.4 = bf16[2,32,1408]{2,1,0:T(8,128)(2,1)S(1)} collective-permute-done((bf16[2,32,1408]{2,1,0:T(8,128)(2,1)S(1)}, bf16[2,32,1408]{2,1,0:T(8,128)(2,1)S(1)}, u32[]{:S(2)}, u32[]{:S(2)}) %collective-permute-start.4) | collective-permute-done | bytes 180256 | tf_op jit(solution)/shard_map/ppermute | solution.py:20
  29.1 4.8 %collective-permute-done.2 = bf16[2,2,32,1280]{3,2,1,0:T(8,128)(2,1)S(1)} collective-permute-done((bf16[2,2,32,1280]{3,2,1,0:T(8,128)(2,1)S(1)}, bf16[2,2,32,1280]{3,2,1,0:T(8,128)(2,1)S(1)}, u32[]{:S(2)}, u32[]{:S(2)}) %collective-permute-start.2) | collective-permute-done | bytes 327712 | tf_op jit(solution)/shard_map/ppermute | solution.py:20
  38.0 3.3 %collective-permute-start.6 = (bf16[2,2,2,32,1408]{4,3,0,1,2:T(8,128)(2,1)S(1)}, bf16[2,2,2,32,1408]{4,3,0,1,2:T(8,128)(2,1)S(1)}, u32[]{:S(2)}, u32[]{:S(2)}) collective-permute-start(bf16[2,2,2,32,1408]{4,3,0,1,2:T(8,128)(2,1)S(1)} %maximum_select_fusion.4), channel_id=1, source_target_pairs={{0,4},{2,6},{4,0},{6,2},{8,12},{10,14},{12,8},{14,10},{16,20},{18,... | collective-permute-start | bytes 2162696 | tf_op jit(solution)/shard_map/ppermute | solution.py:20
  41.6 8.9 %collective-permute-done.3 = bf16[2,2,2,32,1280]{4,3,2,1,0:T(8,128)(2,1)S(1)} collective-permute-done((bf16[2,2,2,32,1280]{4,3,2,1,0:T(8,128)(2,1)S(1)}, bf16[2,2,2,32,1280]{4,3,2,1,0:T(8,128)(2,1)S(1)}, u32[]{:S(2)}, u32[]{:S(2)}) %collective-permute-start.3) | collective-permute-done | bytes 655392 | tf_op jit(solution)/shard_map/ppermute | solution.py:20
  54.3 2.1 %fusion.23 = f32[512,512]{0,1:T(8,128)} fusion(f32[512,512]{1,0:T(8,128)S(1)} %fusion.7, f32[512,512]{1,0:T(8,128)S(1)} %fusion.18, bf16[512,1408]{1,0:T(8,128)(2,1)S(1)} %bitcast.126, bf16[512,4096]{1,0:T(8,128)(2,1)S(1)} %copy-done.7), kind=kOutput, calls=%fused_computation.34 | convolution fusion | flops 738721792 | bytes 6029312 | tf_op jit(solution)/shard_map/dot_general | solution.py:106
  56.4 2.7 %fusion.51 = (bf16[16,144,512]{2,1,0:T(8,128)(2,1)S(1)}, bf16[16,144,512]{2,1,0:T(8,128)(2,1)S(1)}) fusion(bf16[16,448,512]{2,1,0:T(8,128)(2,1)} %param.8), kind=kLoop, calls=%fused_computation.94 | loop fusion | bytes 9437184 | tf_op jit(solution)/shard_map/slice | solution.py:81
  59.4 3.2 %fusion.38 = bf16[512,512,1,1,1]{0,1,4,3,2:T(8,128)(2,1)S(1)} fusion(f32[512,512]{0,1:T(8,128)} %fusion.23, f32[512,512]{0,1:T(8,128)} %collective-permute-done.10), kind=kLoop, calls=%fused_computation.67 | loop fusion | flops 524288 | bytes 2621440 | tf_op jit(solution)/shard_map/convert_element_type | solution.py:110
  68.7 2.0 %slice.35 = bf16[16,160,512]{2,1,0:T(8,128)(2,1)S(1)} slice(bf16[16,448,512]{2,1,0:T(8,128)(2,1)} %param.8), slice={[0:16], [288:448], [0:512]} | slice | bytes 5242880 | tf_op jit(solution)/shard_map/slice | solution.py:81
  70.7 2.0 %convolution_convert_fusion = bf16[2,2,2,160,512]{4,3,2,1,0:T(8,128)(2,1)} fusion(bf16[512,512,1,1,1]{0,1,4,3,2:T(8,128)(2,1)S(1)} %fusion.38, bf16[2,2,2,2,160,512]{5,4,3,2,1,0:T(8,128)(2,1)S(1)} %bitcast.124, s32[]{:T(128)S(6)} %select_n.240), kind=kOutput, calls=%fused_computation.13 | convolution fusion | flops 671744000 | bytes 3145732 | tf_op jit(solution)/shard_map/...kt,tr->...kr/dot_general | solution.py:70
  73.5 19.5 %collective-permute-done.11 = bf16[2,2,2,144,512]{4,3,2,1,0:T(8,128)(2,1)} collective-permute-done((bf16[2,2,2,144,512]{4,3,2,1,0:T(8,128)(2,1)}, bf16[2,2,2,144,512]{4,3,2,1,0:T(8,128)(2,1)}, u32[]{:S(2)}, u32[]{:S(2)}) %collective-permute-start.11) | collective-permute-done | bytes 1179680 | tf_op jit(solution)/shard_map/ppermute | solution.py:20
  93.0 2.6 %convert_add_fusion.2 = f32[2,2,2,144,512]{4,3,2,1,0:T(8,128)S(1)} fusion(bf16[2,2,2,144,512]{4,3,2,1,0:T(8,128)(2,1)} %collective-permute-done.11, bf16[512,512,1,1,1]{0,1,4,3,2:T(8,128)(2,1)S(1)} %fusion.38, bf16[2,2,2,2,144,512]{5,4,3,2,1,0:T(8,128)(2,1)} %bitcast.131, s32[]{:T(128)S(6)} %select_n.237), kind=kOutput, calls=%fused_computation.11 | convolution fusion | flops 605159424 | bytes 5242884 | tf_op jit(solution)/shard_map/...kt,tr->...kr/dot_general | solution.py:70
  97.0 2.1 %convert_add_fusion.1 = f32[2,2,2,144,512]{4,3,2,1,0:T(8,128)S(1)} fusion(bf16[2,2,2,144,512]{4,3,2,1,0:T(8,128)(2,1)} %collective-permute-done.14, bf16[512,512,1,1,1]{0,1,4,3,2:T(8,128)(2,1)S(1)} %fusion.38, bf16[2,2,2,2,144,512]{5,4,3,2,1,0:T(8,128)(2,1)S(1)} %bitcast.129, s32[]{:T(128)S(6)} %select_n.241), kind=kOutput, calls=%fused_computation.10 | convolution fusion | flops 605159424 | bytes 5242884 | tf_op jit(solution)/shard_map/...kt,tr->...kr/dot_general | solution.py:70
  100.6 4.1 %collective-permute-done.17 = bf16[2,2,2,160,512]{4,3,2,1,0:T(8,128)(2,1)} collective-permute-done((bf16[2,2,2,160,512]{4,3,2,1,0:T(8,128)(2,1)}, bf16[2,2,2,160,512]{4,3,2,1,0:T(8,128)(2,1)}, u32[]{:S(2)}, u32[]{:S(2)}) %collective-permute-start.17) | collective-permute-done | bytes 1310752 | tf_op jit(solution)/shard_map/ppermute | solution.py:20
  104.7 2.2 %convert_add_fusion = f32[2,2,2,160,512]{4,3,2,1,0:T(8,128)S(1)} fusion(bf16[2,2,2,160,512]{4,3,2,1,0:T(8,128)(2,1)} %collective-permute-done.17, bf16[512,512,1,1,1]{0,1,4,3,2:T(8,128)(2,1)S(1)} %fusion.38, bf16[2,2,2,2,160,512]{5,4,3,2,1,0:T(8,128)(2,1)S(1)} %bitcast.125, s32[]{:T(128)S(6)} %select_n.239), kind=kOutput, calls=%fused_computation.9 | convolution fusion | flops 672399360 | bytes 5767172 | tf_op jit(solution)/shard_map/...kt,tr->...kr/dot_general | solution.py:70
  108.0 8.1 %collective-permute-done.12 = bf16[2,2,144,512]{3,2,1,0:T(8,128)(2,1)S(1)} collective-permute-done((bf16[2,2,144,512]{3,2,1,0:T(8,128)(2,1)S(1)}, bf16[2,2,144,512]{3,2,1,0:T(8,128)(2,1)S(1)}, u32[]{:S(2)}, u32[]{:S(2)}) %collective-permute-start.12) | collective-permute-done | bytes 589856 | tf_op jit(solution)/shard_map/ppermute | solution.py:20
  118.9 5.8 %collective-permute-done.18 = bf16[2,2,160,512]{3,2,1,0:T(8,128)(2,1)S(1)} collective-permute-done((bf16[2,2,160,512]{3,2,1,0:T(8,128)(2,1)S(1)}, bf16[2,2,160,512]{3,2,1,0:T(8,128)(2,1)S(1)}, u32[]{:S(2)}, u32[]{:S(2)}) %collective-permute-start.18) | collective-permute-done | bytes 655392 | tf_op jit(solution)/shard_map/ppermute | solution.py:20
  128.1 4.0 %collective-permute-done.19 = bf16[2,160,512]{2,1,0:T(8,128)(2,1)S(1)} collective-permute-done((bf16[2,160,512]{2,1,0:T(8,128)(2,1)S(1)}, bf16[2,160,512]{2,1,0:T(8,128)(2,1)S(1)}, u32[]{:S(2)}, u32[]{:S(2)}) %collective-permute-start.19) | collective-permute-done | bytes 327712 | tf_op jit(solution)/shard_map/ppermute | solution.py:20
  133.3 3.3 %collective-permute-start.20 = (bf16[448,512]{1,0:T(8,128)(2,1)}, bf16[448,512]{1,0:T(8,128)(2,1)}, u32[]{:S(2)}, u32[]{:S(2)}) collective-permute-start(bf16[448,512]{1,0:T(8,128)(2,1)} %fusion.39), channel_id=1, source_target_pairs={{0,16},{2,18},{4,20},{6,22},{8,24},{10,26},{12,28},{14,30},{16,0},... | collective-permute-start | bytes 1376264 | tf_op jit(solution)/shard_map/ppermute | solution.py:20
  136.5 13.8 %collective-permute-done.20 = bf16[448,512]{1,0:T(8,128)(2,1)} collective-permute-done((bf16[448,512]{1,0:T(8,128)(2,1)}, bf16[448,512]{1,0:T(8,128)(2,1)}, u32[]{:S(2)}, u32[]{:S(2)}) %collective-permute-start.20) | collective-permute-done | bytes 458784 | tf_op jit(solution)/shard_map/ppermute | solution.py:20
  150.3 3.4 %multiply_convert_fusion = (bf16[448,512]{1,0:T(8,128)(2,1)S(1)}, f32[448,512]{1,0:T(8,128)}, f32[448,512]{1,0:T(8,128)}) fusion(bf16[448,512]{1,0:T(8,128)(2,1)} %collective-permute-done.20, f32[2,448,512]{2,1,0:T(8,128)S(1)} %pad_maximum_fusion, s32[]{:T(128)S(6)} %select_n.243, f32[448,512]{1,0:T(8,128)} %param.13, f32[448,512]{1,0:T(8,128)} %param.12), kind=kLoop, calls=%fused_computation.50 | loop fusion | flops 2523136 | bytes 5505028 | tf_op jit(solution)/shard_map/convert_element_type | solution.py:114
  153.7 2.4 %all_gather.3 = bf16[896,512]{1,0:T(8,128)(2,1)S(1)} all-gather(bf16[448,512]{1,0:T(8,128)(2,1)S(1)} %get-tuple-element.8), channel_id=1, replica_groups=mesh['dp'=16,'fsdp'=2] {'fsdp'}, dimensions={0}, use_global_device_ids=true | all-gather | bytes 1376256 | tf_op jit(solution)/shard_map/all_gather | solution.py:117
  156.2 13.9 %add_convert_fusion = (bf16[4096,896]{1,0:T(8,128)(2,1)}, bf16[4096,896]{1,0:T(8,128)(2,1)}) fusion(bf16[4096,896]{1,0:T(8,128)(2,1)} %param.11, bf16[4096,896]{1,0:T(8,128)(2,1)} %param.10, bf16[896,512]{1,0:T(8,128)(2,1)S(1)} %all_gather.3, bf16[512,1408]{1,0:T(8,128)(2,1)} %bitcast.140, bf16[512,1408]{1,0:T(8,128)(2,1)S(1)} %bitcast.127, ...), kind=kOutput, calls=%fused_computation | convolution fusion | flops 3803709440 | bytes 34471936 | tf_op jit(solution)/shard_map/dot_general | solution.py:115
  (85 shorter events, 35.4 us)
Async XLA Ops:
  0.6 16.2 %collective-permute-start = (bf16[32,4096]{1,0:T(8,128)(2,1)}, bf16[32,4096]{1,0:T(8,128)(2,1)S(1)}, u32[]{:S(2)}, u32[]{:S(2)}) collective-permute-start(bf16[32,4096]{1,0:T(8,128)(2,1)} %bitcast.153), channel_id=1, source_target_pairs={{0,16},{2,18},{4,20},{6,22},{8,24},{10,26},{12,28},{14,30},{16,0},... | collective-permute-start | bytes 786440 | tf_op jit(solution)/shard_map/ppermute | solution.py:20
  18.1 5.5 %collective-permute-start.1 = (bf16[2,32,1280]{2,1,0:T(8,128)(2,1)S(1)}, bf16[2,32,1280]{2,1,0:T(8,128)(2,1)S(1)}, u32[]{:S(2)}, u32[]{:S(2)}) collective-permute-start(bf16[2,32,1280]{2,1,0:T(8,128)(2,1)S(1)} %get-tuple-element.23), channel_id=1, source_target_pairs={{0,4},{2,6},{4,0},{6,2},{8,12},{10,14},{12,8},{14,10},{16,20},{18,... | collective-permute-start | bytes 491528 | tf_op jit(solution)/shard_map/ppermute | solution.py:20
  19.8 8.8 %collective-permute-start.7 = (bf16[2,32,1408]{2,1,0:T(8,128)(2,1)S(1)}, bf16[2,32,1408]{2,1,0:T(8,128)(2,1)S(1)}, u32[]{:S(2)}, u32[]{:S(2)}) collective-permute-start(bf16[2,32,1408]{2,1,0:T(8,128)(2,1)S(1)} %get-tuple-element.19), channel_id=1, source_target_pairs={{0,2},{2,0},{4,6},{6,4},{8,10},{10,8},{12,14},{14,12},{16,18},{18,... | collective-permute-start | bytes 540680 | tf_op jit(solution)/shard_map/ppermute | solution.py:20
  21.4 7.1 %collective-permute-start.4 = (bf16[2,32,1408]{2,1,0:T(8,128)(2,1)S(1)}, bf16[2,32,1408]{2,1,0:T(8,128)(2,1)S(1)}, u32[]{:S(2)}, u32[]{:S(2)}) collective-permute-start(bf16[2,32,1408]{2,1,0:T(8,128)(2,1)S(1)} %get-tuple-element.20), channel_id=1, source_target_pairs={{0,8},{2,10},{4,12},{6,14},{8,0},{10,2},{12,4},{14,6},{16,24},{18,... | collective-permute-start | bytes 540680 | tf_op jit(solution)/shard_map/ppermute | solution.py:20
  23.5 10.3 %collective-permute-start.2 = (bf16[2,2,32,1280]{3,2,1,0:T(8,128)(2,1)S(1)}, bf16[2,2,32,1280]{3,2,1,0:T(8,128)(2,1)S(1)}, u32[]{:S(2)}, u32[]{:S(2)}) collective-permute-start(bf16[2,2,32,1280]{3,2,1,0:T(8,128)(2,1)S(1)} %maximum_select_fusion.13), channel_id=1, source_target_pairs={{0,8},{2,10},{4,12},{6,14},{8,0},{10,2},{12,4},{14,6},{16,24},{18,... | collective-permute-start | bytes 983048 | tf_op jit(solution)/shard_map/ppermute | solution.py:20
  28.8 7.5 %collective-permute-start.8 = (bf16[2,2,32,1408]{3,2,0,1:T(8,128)(2,1)S(1)}, bf16[2,2,32,1408]{3,2,0,1:T(8,128)(2,1)S(1)}, u32[]{:S(2)}, u32[]{:S(2)}) collective-permute-start(bf16[2,2,32,1408]{3,2,0,1:T(8,128)(2,1)S(1)} %maximum_select_fusion.12), channel_id=1, source_target_pairs={{0,4},{2,6},{4,0},{6,2},{8,12},{10,14},{12,8},{14,10},{16,20},{18,... | collective-permute-start | bytes 1081352 | tf_op jit(solution)/shard_map/ppermute | solution.py:20
  29.0 8.8 %collective-permute-start.5 = (bf16[2,2,32,1408]{3,2,0,1:T(8,128)(2,1)S(1)}, bf16[2,2,32,1408]{3,2,0,1:T(8,128)(2,1)S(1)}, u32[]{:S(2)}, u32[]{:S(2)}) collective-permute-start(bf16[2,2,32,1408]{3,2,0,1:T(8,128)(2,1)S(1)} %maximum_select_fusion.10), channel_id=1, source_target_pairs={{0,2},{2,0},{4,6},{6,4},{8,10},{10,8},{12,14},{14,12},{16,18},{18,... | collective-permute-start | bytes 1081352 | tf_op jit(solution)/shard_map/ppermute | solution.py:20
  33.9 16.6 %collective-permute-start.3 = (bf16[2,2,2,32,1280]{4,3,2,1,0:T(8,128)(2,1)S(1)}, bf16[2,2,2,32,1280]{4,3,2,1,0:T(8,128)(2,1)S(1)}, u32[]{:S(2)}, u32[]{:S(2)}) collective-permute-start(bf16[2,2,2,32,1280]{4,3,2,1,0:T(8,128)(2,1)S(1)} %maximum_select_fusion.7), channel_id=1, source_target_pairs={{0,2},{2,0},{4,6},{6,4},{8,10},{10,8},{12,14},{14,12},{16,18},{18,... | collective-permute-start | bytes 1966088 | tf_op jit(solution)/shard_map/ppermute | solution.py:20
  36.5 15.2 %collective-permute-start.9 = (bf16[2,2,2,32,1408]{4,3,0,2,1:T(8,128)(2,1)S(1)}, bf16[2,2,2,32,1408]{4,3,0,2,1:T(8,128)(2,1)S(1)}, u32[]{:S(2)}, u32[]{:S(2)}) collective-permute-start(bf16[2,2,2,32,1408]{4,3,0,2,1:T(8,128)(2,1)S(1)} %maximum_select_fusion.6), channel_id=1, source_target_pairs={{0,8},{2,10},{4,12},{6,14},{8,0},{10,2},{12,4},{14,6},{16,24},{18,... | collective-permute-start | bytes 2162696 | tf_op jit(solution)/shard_map/ppermute | solution.py:20
  38.0 14.5 %collective-permute-start.6 = (bf16[2,2,2,32,1408]{4,3,0,1,2:T(8,128)(2,1)S(1)}, bf16[2,2,2,32,1408]{4,3,0,1,2:T(8,128)(2,1)S(1)}, u32[]{:S(2)}, u32[]{:S(2)}) collective-permute-start(bf16[2,2,2,32,1408]{4,3,0,1,2:T(8,128)(2,1)S(1)} %maximum_select_fusion.4), channel_id=1, source_target_pairs={{0,4},{2,6},{4,0},{6,2},{8,12},{10,14},{12,8},{14,10},{16,20},{18,... | collective-permute-start | bytes 2162696 | tf_op jit(solution)/shard_map/ppermute | solution.py:20
  41.3 9.4 %copy-start.7 = (bf16[512,4096]{1,0:T(8,128)(2,1)S(1)}, bf16[512,4096]{1,0:T(8,128)(2,1)}, u32[]{:S(2)}) copy-start(bf16[512,4096]{1,0:T(8,128)(2,1)} %param.7) | copy-start | bytes 12582916
  56.4 3.0 %collective-permute-start.10 = (f32[512,512]{0,1:T(8,128)}, f32[512,512]{0,1:T(8,128)}, u32[]{:S(2)}, u32[]{:S(2)}) collective-permute-start(f32[512,512]{0,1:T(8,128)} %fusion.23), channel_id=1, source_target_pairs={{0,1},{1,0},{2,3},{3,2},{4,5},{5,4},{6,7},{7,6},{8,9},{9,8},{10,11... | collective-permute-start | bytes 3145736 | tf_op jit(solution)/shard_map/ppermute | solution.py:95
  59.2 6.6 %copy-start.2 = (bf16[16,144,512]{2,1,0:T(8,128)(2,1)}, bf16[16,144,512]{2,1,0:T(8,128)(2,1)S(1)}, u32[]{:S(2)}) copy-start(bf16[16,144,512]{2,1,0:T(8,128)(2,1)S(1)} %get-tuple-element.14) | copy-start | bytes 7077892
  64.4 28.6 %collective-permute-start.11 = (bf16[2,2,2,144,512]{4,3,2,1,0:T(8,128)(2,1)}, bf16[2,2,2,144,512]{4,3,2,1,0:T(8,128)(2,1)}, u32[]{:S(2)}, u32[]{:S(2)}) collective-permute-start(bf16[2,2,2,144,512]{4,3,2,1,0:T(8,128)(2,1)} %convolution_convert_fusion.2), channel_id=1, source_target_pairs={{0,2},{2,0},{4,6},{6,4},{8,10},{10,8},{12,14},{14,12},{16,18},{18,... | collective-permute-start | bytes 3538952 | tf_op jit(solution)/shard_map/ppermute | solution.py:20
  67.6 29.3 %collective-permute-start.14 = (bf16[2,2,2,144,512]{4,3,2,1,0:T(8,128)(2,1)}, bf16[2,2,2,144,512]{4,3,2,1,0:T(8,128)(2,1)}, u32[]{:S(2)}, u32[]{:S(2)}) collective-permute-start(bf16[2,2,2,144,512]{4,3,2,1,0:T(8,128)(2,1)} %convolution_convert_fusion.1), channel_id=1, source_target_pairs={{0,4},{2,6},{4,0},{6,2},{8,12},{10,14},{12,8},{14,10},{16,20},{18,... | collective-permute-start | bytes 3538952 | tf_op jit(solution)/shard_map/ppermute | solution.py:20
  72.7 32.0 %collective-permute-start.17 = (bf16[2,2,2,160,512]{4,3,2,1,0:T(8,128)(2,1)}, bf16[2,2,2,160,512]{4,3,2,1,0:T(8,128)(2,1)}, u32[]{:S(2)}, u32[]{:S(2)}) collective-permute-start(bf16[2,2,2,160,512]{4,3,2,1,0:T(8,128)(2,1)} %convolution_convert_fusion), channel_id=1, source_target_pairs={{0,8},{2,10},{4,12},{6,14},{8,0},{10,2},{12,4},{14,6},{16,24},{18,... | collective-permute-start | bytes 3932168 | tf_op jit(solution)/shard_map/ppermute | solution.py:20
  95.7 20.4 %collective-permute-start.12 = (bf16[2,2,144,512]{3,2,1,0:T(8,128)(2,1)S(1)}, bf16[2,2,144,512]{3,2,1,0:T(8,128)(2,1)S(1)}, u32[]{:S(2)}, u32[]{:S(2)}) collective-permute-start(bf16[2,2,144,512]{3,2,1,0:T(8,128)(2,1)S(1)} %fusion.36), channel_id=1, source_target_pairs={{0,8},{2,10},{4,12},{6,14},{8,0},{10,2},{12,4},{14,6},{16,24},{18,... | collective-permute-start | bytes 1769480 | tf_op jit(solution)/shard_map/ppermute | solution.py:20
  99.2 18.3 %collective-permute-start.15 = (bf16[2,2,144,512]{3,2,1,0:T(8,128)(2,1)S(1)}, bf16[2,2,144,512]{3,2,1,0:T(8,128)(2,1)S(1)}, u32[]{:S(2)}, u32[]{:S(2)}) collective-permute-start(bf16[2,2,144,512]{3,2,1,0:T(8,128)(2,1)S(1)} %fusion.37), channel_id=1, source_target_pairs={{0,2},{2,0},{4,6},{6,4},{8,10},{10,8},{12,14},{14,12},{16,18},{18,... | collective-permute-start | bytes 1769480 | tf_op jit(solution)/shard_map/ppermute | solution.py:20
  107.0 17.7 %collective-permute-start.18 = (bf16[2,2,160,512]{3,2,1,0:T(8,128)(2,1)S(1)}, bf16[2,2,160,512]{3,2,1,0:T(8,128)(2,1)S(1)}, u32[]{:S(2)}, u32[]{:S(2)}) collective-permute-start(bf16[2,2,160,512]{3,2,1,0:T(8,128)(2,1)S(1)} %fusion.35), channel_id=1, source_target_pairs={{0,4},{2,6},{4,0},{6,2},{8,12},{10,14},{12,8},{14,10},{16,20},{18,... | collective-permute-start | bytes 1966088 | tf_op jit(solution)/shard_map/ppermute | solution.py:20
  116.4 11.5 %collective-permute-start.13 = (bf16[2,144,512]{2,1,0:T(8,128)(2,1)S(1)}, bf16[2,144,512]{2,1,0:T(8,128)(2,1)S(1)}, u32[]{:S(2)}, u32[]{:S(2)}) collective-permute-start(bf16[2,144,512]{2,1,0:T(8,128)(2,1)S(1)} %fusion.41), channel_id=1, source_target_pairs={{0,4},{2,6},{4,0},{6,2},{8,12},{10,14},{12,8},{14,10},{16,20},{18,... | collective-permute-start | bytes 884744 | tf_op jit(solution)/shard_map/ppermute | solution.py:20
  117.7 10.3 %collective-permute-start.16 = (bf16[2,144,512]{2,1,0:T(8,128)(2,1)S(1)}, bf16[2,144,512]{2,1,0:T(8,128)(2,1)S(1)}, u32[]{:S(2)}, u32[]{:S(2)}) collective-permute-start(bf16[2,144,512]{2,1,0:T(8,128)(2,1)S(1)} %fusion.42), channel_id=1, source_target_pairs={{0,8},{2,10},{4,12},{6,14},{8,0},{10,2},{12,4},{14,6},{16,24},{18,... | collective-permute-start | bytes 884744 | tf_op jit(solution)/shard_map/ppermute | solution.py:20
  125.0 7.1 %collective-permute-start.19 = (bf16[2,160,512]{2,1,0:T(8,128)(2,1)S(1)}, bf16[2,160,512]{2,1,0:T(8,128)(2,1)S(1)}, u32[]{:S(2)}, u32[]{:S(2)}) collective-permute-start(bf16[2,160,512]{2,1,0:T(8,128)(2,1)S(1)} %fusion.40), channel_id=1, source_target_pairs={{0,2},{2,0},{4,6},{6,4},{8,10},{10,8},{12,14},{14,12},{16,18},{18,... | collective-permute-start | bytes 983048 | tf_op jit(solution)/shard_map/ppermute | solution.py:20
  133.3 17.1 %collective-permute-start.20 = (bf16[448,512]{1,0:T(8,128)(2,1)}, bf16[448,512]{1,0:T(8,128)(2,1)}, u32[]{:S(2)}, u32[]{:S(2)}) collective-permute-start(bf16[448,512]{1,0:T(8,128)(2,1)} %fusion.39), channel_id=1, source_target_pairs={{0,16},{2,18},{4,20},{6,22},{8,24},{10,26},{12,28},{14,30},{16,0},... | collective-permute-start | bytes 1376264 | tf_op jit(solution)/shard_map/ppermute | solution.py:20
  136.5 19.6 %copy-start.1 = (bf16[2,2,2,2,32,1408]{5,4,3,2,1,0:T(8,128)(2,1)S(1)}, bf16[2,2,2,2,32,1408]{5,4,3,2,1,0:T(8,128)(2,1)}, u32[]{:S(2)}) copy-start(bf16[2,2,2,2,32,1408]{5,4,3,2,1,0:T(8,128)(2,1)} %copy-done) | copy-start | bytes 4325380
  (5 other events, 12.9 us)

commit v3 on v2

--- a/solution.py
+++ b/solution.py
@@ -12,7 +12,7 @@
         return [(0, whole)]
     count, total, ends = whole // unit, sum(SHARES), [0]
     for at in range(len(SHARES)):
-        ends.append(count * sum(SHARES[: at + 1]) // total)
+        ends.append(-(-count * sum(SHARES[: at + 1]) // total))
     return [(low * unit, high * unit) for low, high in zip(ends, ends[1:]) if high > low]
 
 
@@ -50,7 +50,13 @@
                 part, grads = lax.optimization_barrier((part, grads))
             part = grown(part, bit, done, size)
         parts.append(part.reshape(-1, end - start))
-    return cuts, parts, grads
+    slices = []
+    for order, (start, end) in zip(orders, pieces(grads.shape[1], 16)):
+        part = grads[:, start:end].reshape((2,) * bits + (end - start, grads.shape[2]))
+        axis, mine = bits - 1 - order[0], bit_of(order[0])
+        slices.append([lax.dynamic_index_in_dim(part, which, axis, keepdims=False) for which in (mine, 1 - mine)])
+    parts[0], slices = lax.optimization_barrier((parts[0], slices))
+    return cuts, parts, slices
 
 
 def shrunk(held, bit, left, size):
@@ -61,24 +67,21 @@
     return keep + swap(give.astype(jnp.bfloat16), bit, size).astype(jnp.float32)
 
 
-def started(grads, projected, bit, left, size):
-    axis, mine = left.index(bit), bit_of(bit)
+def started(halves, projected, bit, left, size):
     left.remove(bit)
 
-    def term(which, kind):
-        part = lax.dynamic_index_in_dim(grads, which, axis, keepdims=False)
+    def term(part, kind):
         out = jnp.einsum("...kt,tr->...kr", part, projected, preferred_element_type=jnp.float32)
         return out.astype(kind)
 
-    other = swap(term(1 - mine, jnp.bfloat16), bit, size)
-    return term(mine, jnp.float32) + other.astype(jnp.float32)
+    other = swap(term(halves[1], jnp.bfloat16), bit, size)
+    return term(halves[0], jnp.float32) + other.astype(jnp.float32)
 
 
 def scattered(grads, projected, bits, size):
     orders, shared = turns(bits)
     sums = []
-    for at, (start, end) in enumerate(pieces(grads.shape[1], 16)):
-        part = grads[:, start:end].reshape((2,) * bits + (end - start, grads.shape[2]))
+    for at, part in enumerate(grads):
         left = list(range(bits))[::-1]
         held = started(part, projected, orders[at][0], left, size)
         for bit in orders[at][1:]:
@@ -100,7 +103,7 @@
     bits = size.bit_length() - 1
 
     def on_device(activations, out_grads, proj_basis, weight, ema_weight, first_moment, second_moment):
-        cuts, columns, out_grads = gathered(proj_basis.T, bits, size, out_grads)
+        cuts, columns, grads = gathered(proj_basis.T, bits, size, out_grads)
         partial_value = 0.0
         for (low, high), part in zip(cuts, columns):
             partial_value += lax.dot_general(
@@ -108,7 +111,7 @@
             )
         full_basis = jnp.concatenate(columns, axis=1)
         projected = summed(partial_value, devices).astype(jnp.bfloat16)
-        proj_grads = scattered(out_grads, projected, bits, size)
+        proj_grads = scattered(grads, projected, bits, size)
         new_first = 0.9 * first_moment + 0.1 * proj_grads
         new_second = 0.95 * second_moment + 0.05 * proj_grads * proj_grads
         direction = (new_first / jnp.sqrt(new_second)).astype(jnp.bfloat16)

time: 170 us -> 165 us (0.971)
  starting transfers between devices: 29 us -> 25.6 us
  local copies, waits for them, and re-layouts: 7.05 us -> 10.1 us
  other arithmetic: 10.4 us -> 7.51 us
    ppermute x20, starting transfers between devices: 29 us -> 25.6 us  [swap(): return lax.ppermute(value, 'dp', [(i, i ^ 1 << bit) for i in range(size)])]
    ppermute x20, waiting for transfers between devices: 89.4 us -> 86.3 us  [swap(): return lax.ppermute(value, 'dp', [(i, i ^ 1 << bit) for i in range(size)])]
    unnamed x16, local copies, waits for them, and re-layouts: 0.61 us -> 3.65 us
    convert_element_type x1, other arithmetic: 3.15 us -> 0.26 us  [on_device(): projected = summed(partial_value, devices).astype(jnp.bfloat16)]
    squeeze x0 -> x3, local copies, waits for them, and re-layouts: none -> 2.74 us  [gathered(): lax.dynamic_index_in_dim(part, which, axis, keepdims=False)]
    slice x2 -> x3, local copies, waits for them, and re-layouts: 4.74 us -> 2.12 us  [gathered(): grads[:, start:end].reshape((2,) * bits + (end - start, grads.shape[2]))]
    ppermute x1, waiting for transfers between devices: 0.22 us -> 2.65 us  [summed(): return value + lax.ppermute(value, 'fsdp', [(0, 1), (1, 0)])]
  transfers between devices with their start and end apart: 21 -> 21, of which waited for: 16 -> 15; matrix products, arithmetic and copies ran while one was open for 11% -> 11% of each run, Pallas kernels for 0% -> 0%
where the time goes in v3:
time: 165 us
  waiting for transfers between devices  89 us (54%)
  matrix products  29.1 us (18%)
  starting transfers between devices  25.6 us (16%)
  local copies, waits for them, and re-layouts  10.1 us (6%)
  other arithmetic  7.51 us (5%)
  blocking collectives  2.58 us (2%)
    ppermute x20, waiting for transfers between devices, swap(): return lax.ppermute(value, 'dp', [(i, i ^ 1 << bit) for i in range(size)])  86.3 us
    ppermute x20, starting transfers between devices, swap(): return lax.ppermute(value, 'dp', [(i, i ^ 1 << bit) for i in range(size)])  25.6 us
    dot_general x1, matrix products, on_device(): lax.dot_general(full_basis, lax.all_gather(direction, 'fsdp', axis=0, til...  13.7 us
    dot_general x6, matrix products, term(): jnp.einsum('...kt,tr->...kr', part, projected, preferred_element_type=jnp...  12.5 us
    unnamed x16, local copies, waits for them, and re-layouts  3.65 us
    convert_element_type x1, other arithmetic, on_device(): direction = (new_first / jnp.sqrt(new_second)).astype(jnp.bfloat16)  3.4 us
  transfers between devices with their start and end apart: 21, of which 15 were waited for; matrix products, arithmetic and copies ran while one was open for 11% of the time, Pallas kernels for 0%

profile of v3, /device:TPU:0, one launch (start us, length us, event | category | flops | bytes accessed | tf_op | source)
XLA Modules:
  0.0 165.1 jit_solution(2354165845346762161)
XLA Ops:
  0.6 4.1 %collective-permute-start = (bf16[32,4096]{1,0:T(8,128)(2,1)}, bf16[32,4096]{1,0:T(8,128)(2,1)S(1)}, u32[]{:S(2)}, u32[]{:S(2)}) collective-permute-start(bf16[32,4096]{1,0:T(8,128)(2,1)} %bitcast.145), channel_id=1, source_target_pairs={{0,16},{2,18},{4,20},{6,22},{8,24},{10,26},{12,28},{14,30},{16,0},... | collective-permute-start | bytes 786440 | tf_op jit(solution)/shard_map/ppermute | solution.py:20
  4.7 12.1 %collective-permute-done = bf16[32,4096]{1,0:T(8,128)(2,1)S(1)} collective-permute-done((bf16[32,4096]{1,0:T(8,128)(2,1)}, bf16[32,4096]{1,0:T(8,128)(2,1)S(1)}, u32[]{:S(2)}, u32[]{:S(2)}) %collective-permute-start) | collective-permute-done | bytes 262176 | tf_op jit(solution)/shard_map/ppermute | solution.py:20
  25.2 2.9 %collective-permute-done.1 = bf16[2,32,1408]{2,1,0:T(8,128)(2,1)S(1)} collective-permute-done((bf16[2,32,1408]{2,1,0:T(8,128)(2,1)S(1)}, bf16[2,32,1408]{2,1,0:T(8,128)(2,1)S(1)}, u32[]{:S(2)}, u32[]{:S(2)}) %collective-permute-start.1) | collective-permute-done | bytes 180256 | tf_op jit(solution)/shard_map/ppermute | solution.py:20
  29.2 4.4 %collective-permute-done.8 = bf16[2,2,32,1280]{3,2,0,1:T(8,128)(2,1)S(1)} collective-permute-done((bf16[2,2,32,1280]{3,2,0,1:T(8,128)(2,1)S(1)}, bf16[2,2,32,1280]{3,2,0,1:T(8,128)(2,1)S(1)}, u32[]{:S(2)}, u32[]{:S(2)}) %collective-permute-start.8) | collective-permute-done | bytes 327712 | tf_op jit(solution)/shard_map/ppermute | solution.py:20
  43.9 5.8 %collective-permute-done.9 = bf16[2,2,2,32,1280]{4,3,0,2,1:T(8,128)(2,1)S(1)} collective-permute-done((bf16[2,2,2,32,1280]{4,3,0,2,1:T(8,128)(2,1)S(1)}, bf16[2,2,2,32,1280]{4,3,0,2,1:T(8,128)(2,1)S(1)}, u32[]{:S(2)}, u32[]{:S(2)}) %collective-permute-start.9) | collective-permute-done | bytes 655392 | tf_op jit(solution)/shard_map/ppermute | solution.py:20
  50.0 2.3 %copy-done.5 = bf16[512,4096]{1,0:T(8,128)(2,1)S(1)} copy-done((bf16[512,4096]{1,0:T(8,128)(2,1)S(1)}, bf16[512,4096]{1,0:T(8,128)(2,1)}, u32[]{:S(2)}) %copy-start.5) | copy-done | bytes 4194328
  56.1 2.6 %collective-permute-done.10 = f32[512,512]{0,1:T(8,128)S(1)} collective-permute-done((f32[512,512]{0,1:T(8,128)S(1)}, f32[512,512]{0,1:T(8,128)S(1)}, u32[]{:S(2)}, u32[]{:S(2)}) %collective-permute-start.10) | collective-permute-done | bytes 1048608 | tf_op jit(solution)/shard_map/ppermute | solution.py:98
  61.3 1.9 %convolution_convert_fusion.2 = bf16[2,2,2,144,512]{4,3,0,1,2:T(8,128)(2,1)} fusion(bf16[2,2,2,144,512]{4,3,2,1,0:T(8,128)(2,1)S(1)} %get-tuple-element.19, bf16[512,512]{0,1:T(8,128)(2,1)S(1)} %add_convert_fusion.1), kind=kOutput, calls=%fused_computation.15 | convolution fusion | flops 604569600 | bytes 2883584 | tf_op jit(solution)/shard_map/...kt,tr->...kr/dot_general | solution.py:74
  64.5 2.0 %convolution_convert_fusion = bf16[2,2,2,160,512]{4,3,2,1,0:T(8,128)(2,1)} fusion(bf16[2,2,2,160,512]{4,3,2,1,0:T(8,128)(2,1)S(1)} %get-tuple-element.17, bf16[512,512]{0,1:T(8,128)(2,1)S(1)} %add_convert_fusion.1), kind=kOutput, calls=%fused_computation.13 | convolution fusion | flops 671744000 | bytes 3145728 | tf_op jit(solution)/shard_map/...kt,tr->...kr/dot_general | solution.py:74
  67.3 21.9 %collective-permute-done.17 = bf16[2,2,2,144,512]{4,3,0,2,1:T(8,128)(2,1)} collective-permute-done((bf16[2,2,2,144,512]{4,3,0,2,1:T(8,128)(2,1)}, bf16[2,2,2,144,512]{4,3,0,2,1:T(8,128)(2,1)}, u32[]{:S(2)}, u32[]{:S(2)}) %collective-permute-start.17) | collective-permute-done | bytes 1179680 | tf_op jit(solution)/shard_map/ppermute | solution.py:20
  89.2 2.4 %convert_add_fusion.1 = f32[2,2,2,144,512]{4,3,0,2,1:T(8,128)S(1)} fusion(bf16[2,2,2,144,512]{4,3,0,2,1:T(8,128)(2,1)} %collective-permute-done.17, bf16[2,2,2,144,512]{4,3,2,1,0:T(8,128)(2,1)} %get-tuple-element.20, bf16[512,512]{0,1:T(8,128)(2,1)S(1)} %add_convert_fusion.1), kind=kOutput, calls=%fused_computation.10 | convolution fusion | flops 605159424 | bytes 5242880 | tf_op jit(solution)/shard_map/...kt,tr->...kr/dot_general | solution.py:74
  93.3 2.1 %convert_add_fusion.2 = f32[2,2,2,144,512]{4,3,0,1,2:T(8,128)S(1)} fusion(bf16[2,2,2,144,512]{4,3,0,1,2:T(8,128)(2,1)} %collective-permute-done.14, bf16[2,2,2,144,512]{4,3,2,1,0:T(8,128)(2,1)S(1)} %copy-done.1, bf16[512,512]{0,1:T(8,128)(2,1)S(1)} %add_convert_fusion.1), kind=kOutput, calls=%fused_computation.11 | convolution fusion | flops 605159424 | bytes 5242880 | tf_op jit(solution)/shard_map/...kt,tr->...kr/dot_general | solution.py:74
  97.1 2.2 %convert_add_fusion = f32[2,2,2,160,512]{4,3,2,1,0:T(8,128)S(1)} fusion(bf16[2,2,2,160,512]{4,3,2,1,0:T(8,128)(2,1)} %collective-permute-done.11, bf16[2,2,2,160,512]{4,3,2,1,0:T(8,128)(2,1)S(1)} %get-tuple-element.16, bf16[512,512]{0,1:T(8,128)(2,1)S(1)} %add_convert_fusion.1), kind=kOutput, calls=%fused_computation.9 | convolution fusion | flops 672399360 | bytes 5767168 | tf_op jit(solution)/shard_map/...kt,tr->...kr/dot_general | solution.py:74
  99.4 2.9 %collective-permute-start.12 = (bf16[2,2,160,512]{3,2,1,0:T(8,128)(2,1)S(1)}, bf16[2,2,160,512]{3,2,1,0:T(8,128)(2,1)S(1)}, u32[]{:S(2)}, u32[]{:S(2)}) collective-permute-start(bf16[2,2,160,512]{3,2,1,0:T(8,128)(2,1)S(1)} %fusion.27), channel_id=1, source_target_pairs={{0,8},{2,10},{4,12},{6,14},{8,0},{10,2},{12,4},{14,6},{16,24},{18,... | collective-permute-start | bytes 1966088 | tf_op jit(solution)/shard_map/ppermute | solution.py:20
  102.3 4.0 %collective-permute-done.18 = bf16[2,2,144,512]{3,2,0,1:T(8,128)(2,1)S(1)} collective-permute-done((bf16[2,2,144,512]{3,2,0,1:T(8,128)(2,1)S(1)}, bf16[2,2,144,512]{3,2,0,1:T(8,128)(2,1)S(1)}, u32[]{:S(2)}, u32[]{:S(2)}) %collective-permute-start.18) | collective-permute-done | bytes 589856 | tf_op jit(solution)/shard_map/ppermute | solution.py:20
  107.2 4.7 %collective-permute-done.15 = bf16[2,2,144,512]{3,2,0,1:T(8,128)(2,1)S(1)} collective-permute-done((bf16[2,2,144,512]{3,2,0,1:T(8,128)(2,1)S(1)}, bf16[2,2,144,512]{3,2,0,1:T(8,128)(2,1)S(1)}, u32[]{:S(2)}, u32[]{:S(2)}) %collective-permute-start.15) | collective-permute-done | bytes 589856 | tf_op jit(solution)/shard_map/ppermute | solution.py:20
  112.8 5.2 %collective-permute-done.12 = bf16[2,2,160,512]{3,2,1,0:T(8,128)(2,1)S(1)} collective-permute-done((bf16[2,2,160,512]{3,2,1,0:T(8,128)(2,1)S(1)}, bf16[2,2,160,512]{3,2,1,0:T(8,128)(2,1)S(1)}, u32[]{:S(2)}, u32[]{:S(2)}) %collective-permute-start.12) | collective-permute-done | bytes 655392 | tf_op jit(solution)/shard_map/ppermute | solution.py:20
  118.4 2.8 %collective-permute-done.16 = bf16[2,144,512]{2,1,0:T(8,128)(2,1)S(1)} collective-permute-done((bf16[2,144,512]{2,1,0:T(8,128)(2,1)S(1)}, bf16[2,144,512]{2,1,0:T(8,128)(2,1)S(1)}, u32[]{:S(2)}, u32[]{:S(2)}) %collective-permute-start.16) | collective-permute-done | bytes 294944 | tf_op jit(solution)/shard_map/ppermute | solution.py:20
  121.3 4.0 %collective-permute-done.13 = bf16[2,160,512]{2,1,0:T(8,128)(2,1)S(1)} collective-permute-done((bf16[2,160,512]{2,1,0:T(8,128)(2,1)S(1)}, bf16[2,160,512]{2,1,0:T(8,128)(2,1)S(1)}, u32[]{:S(2)}, u32[]{:S(2)}) %collective-permute-start.13) | collective-permute-done | bytes 327712 | tf_op jit(solution)/shard_map/ppermute | solution.py:20
  127.9 3.2 %collective-permute-start.20 = (bf16[448,512]{1,0:T(8,128)(2,1)}, bf16[448,512]{1,0:T(8,128)(2,1)S(1)}, u32[]{:S(2)}, u32[]{:S(2)}) collective-permute-start(bf16[448,512]{1,0:T(8,128)(2,1)} %fusion.36), channel_id=1, source_target_pairs={{0,16},{2,18},{4,20},{6,22},{8,24},{10,26},{12,28},{14,30},{16,0},... | collective-permute-start | bytes 1376264 | tf_op jit(solution)/shard_map/ppermute | solution.py:20
  131.1 14.4 %collective-permute-done.20 = bf16[448,512]{1,0:T(8,128)(2,1)S(1)} collective-permute-done((bf16[448,512]{1,0:T(8,128)(2,1)}, bf16[448,512]{1,0:T(8,128)(2,1)S(1)}, u32[]{:S(2)}, u32[]{:S(2)}) %collective-permute-start.20) | collective-permute-done | bytes 458784 | tf_op jit(solution)/shard_map/ppermute | solution.py:20
  145.4 3.4 %multiply_convert_fusion = (bf16[448,512]{1,0:T(8,128)(2,1)S(1)}, f32[448,512]{1,0:T(8,128)}, f32[448,512]{1,0:T(8,128)}) fusion(bf16[448,512]{1,0:T(8,128)(2,1)S(1)} %collective-permute-done.20, f32[2,448,512]{2,1,0:T(8,128)} %copy-done, s32[]{:T(128)S(6)} %select_n.243, f32[448,512]{1,0:T(8,128)} %param.13, f32[448,512]{1,0:T(8,128)} %param.12), kind=kLoop, calls=%fused_computation.48 | loop fusion | flops 2523136 | bytes 5505028 | tf_op jit(solution)/shard_map/convert_element_type | solution.py:117
  148.8 2.6 %all_gather.3 = bf16[896,512]{1,0:T(8,128)(2,1)} all-gather(bf16[448,512]{1,0:T(8,128)(2,1)S(1)} %get-tuple-element.22), channel_id=1, replica_groups=mesh['dp'=16,'fsdp'=2] {'fsdp'}, dimensions={0}, use_global_device_ids=true | all-gather | bytes 1376256 | tf_op jit(solution)/shard_map/all_gather | solution.py:120
  151.4 13.7 %add_convert_fusion = (bf16[4096,896]{1,0:T(8,128)(2,1)}, bf16[4096,896]{1,0:T(8,128)(2,1)}) fusion(bf16[4096,896]{1,0:T(8,128)(2,1)} %param.11, bf16[4096,896]{1,0:T(8,128)(2,1)} %param.10, bf16[896,512]{1,0:T(8,128)(2,1)} %all_gather.3, bf16[512,1280]{1,0:T(8,128)(2,1)} %bitcast.136, bf16[512,1408]{1,0:T(8,128)(2,1)S(1)} %bitcast.123, ...), kind=kOutput, calls=%fused_computation | convolution fusion | flops 3803709440 | bytes 34471936 | tf_op jit(solution)/shard_map/dot_general | solution.py:118
  (90 shorter events, 36.3 us)
Async XLA Ops:
  0.6 16.2 %collective-permute-start = (bf16[32,4096]{1,0:T(8,128)(2,1)}, bf16[32,4096]{1,0:T(8,128)(2,1)S(1)}, u32[]{:S(2)}, u32[]{:S(2)}) collective-permute-start(bf16[32,4096]{1,0:T(8,128)(2,1)} %bitcast.145), channel_id=1, source_target_pairs={{0,16},{2,18},{4,20},{6,22},{8,24},{10,26},{12,28},{14,30},{16,0},... | collective-permute-start | bytes 786440 | tf_op jit(solution)/shard_map/ppermute | solution.py:20
  18.1 5.5 %collective-permute-start.7 = (bf16[2,32,1280]{2,1,0:T(8,128)(2,1)S(1)}, bf16[2,32,1280]{2,1,0:T(8,128)(2,1)S(1)}, u32[]{:S(2)}, u32[]{:S(2)}) collective-permute-start(bf16[2,32,1280]{2,1,0:T(8,128)(2,1)S(1)} %get-tuple-element.43), channel_id=1, source_target_pairs={{0,2},{2,0},{4,6},{6,4},{8,10},{10,8},{12,14},{14,12},{16,18},{18,... | collective-permute-start | bytes 491528 | tf_op jit(solution)/shard_map/ppermute | solution.py:20
  19.7 19.2 %slice-start = ((s8[7340032]{0:T(1024)(128)(4,1)}), s8[4194304]{0:T(1024)(128)(4,1)S(1)}, s32[]{:S(2)}) async-start(s8[7340032]{0:T(1024)(128)(4,1)} %bitcast.117), calls=%async_computation | async-start | bytes 8388608
  19.8 8.5 %collective-permute-start.4 = (bf16[2,32,1408]{2,1,0:T(8,128)(2,1)S(1)}, bf16[2,32,1408]{2,1,0:T(8,128)(2,1)S(1)}, u32[]{:S(2)}, u32[]{:S(2)}) collective-permute-start(bf16[2,32,1408]{2,1,0:T(8,128)(2,1)S(1)} %get-tuple-element.39), channel_id=1, source_target_pairs={{0,8},{2,10},{4,12},{6,14},{8,0},{10,2},{12,4},{14,6},{16,24},{18,... | collective-permute-start | bytes 540680 | tf_op jit(solution)/shard_map/ppermute | solution.py:20
  20.6 7.5 %collective-permute-start.1 = (bf16[2,32,1408]{2,1,0:T(8,128)(2,1)S(1)}, bf16[2,32,1408]{2,1,0:T(8,128)(2,1)S(1)}, u32[]{:S(2)}, u32[]{:S(2)}) collective-permute-start(bf16[2,32,1408]{2,1,0:T(8,128)(2,1)S(1)} %get-tuple-element.40), channel_id=1, source_target_pairs={{0,4},{2,6},{4,0},{6,2},{8,12},{10,14},{12,8},{14,10},{16,20},{18,... | collective-permute-start | bytes 540680 | tf_op jit(solution)/shard_map/ppermute | solution.py:20
  23.5 10.0 %collective-permute-start.8 = (bf16[2,2,32,1280]{3,2,0,1:T(8,128)(2,1)S(1)}, bf16[2,2,32,1280]{3,2,0,1:T(8,128)(2,1)S(1)}, u32[]{:S(2)}, u32[]{:S(2)}) collective-permute-start(bf16[2,2,32,1280]{3,2,0,1:T(8,128)(2,1)S(1)} %maximum_select_fusion.13), channel_id=1, source_target_pairs={{0,4},{2,6},{4,0},{6,2},{8,12},{10,14},{12,8},{14,10},{16,20},{18,... | collective-permute-start | bytes 983048 | tf_op jit(solution)/shard_map/ppermute | solution.py:20
  28.2 8.2 %collective-permute-start.2 = (bf16[2,2,32,1408]{3,2,1,0:T(8,128)(2,1)S(1)}, bf16[2,2,32,1408]{3,2,1,0:T(8,128)(2,1)S(1)}, u32[]{:S(2)}, u32[]{:S(2)}) collective-permute-start(bf16[2,2,32,1408]{3,2,1,0:T(8,128)(2,1)S(1)} %maximum_select_fusion.9), channel_id=1, source_target_pairs={{0,8},{2,10},{4,12},{6,14},{8,0},{10,2},{12,4},{14,6},{16,24},{18,... | collective-permute-start | bytes 1081352 | tf_op jit(solution)/shard_map/ppermute | solution.py:20
  28.3 8.8 %collective-permute-start.5 = (bf16[2,2,32,1408]{3,2,0,1:T(8,128)(2,1)S(1)}, bf16[2,2,32,1408]{3,2,0,1:T(8,128)(2,1)S(1)}, u32[]{:S(2)}, u32[]{:S(2)}) collective-permute-start(bf16[2,2,32,1408]{3,2,0,1:T(8,128)(2,1)S(1)} %maximum_select_fusion.11), channel_id=1, source_target_pairs={{0,2},{2,0},{4,6},{6,4},{8,10},{10,8},{12,14},{14,12},{16,18},{18,... | collective-permute-start | bytes 1081352 | tf_op jit(solution)/shard_map/ppermute | solution.py:20
  29.0 9.9 %slice-start.1 = ((s8[7340032]{0:T(1024)(128)(4,1)}), s8[3145728]{0:T(1024)(128)(4,1)S(1)}, s32[]{:S(2)}) async-start(s8[7340032]{0:T(1024)(128)(4,1)} %bitcast.117), calls=%async_computation.1 | async-start | bytes 6291456
  33.7 16.0 %collective-permute-start.9 = (bf16[2,2,2,32,1280]{4,3,0,2,1:T(8,128)(2,1)S(1)}, bf16[2,2,2,32,1280]{4,3,0,2,1:T(8,128)(2,1)S(1)}, u32[]{:S(2)}, u32[]{:S(2)}) collective-permute-start(bf16[2,2,2,32,1280]{4,3,0,2,1:T(8,128)(2,1)S(1)} %maximum_select_fusion.7), channel_id=1, source_target_pairs={{0,8},{2,10},{4,12},{6,14},{8,0},{10,2},{12,4},{14,6},{16,24},{18,... | collective-permute-start | bytes 1966088 | tf_op jit(solution)/shard_map/ppermute | solution.py:20
  36.5 17.2 %collective-permute-start.3 = (bf16[2,2,2,32,1408]{4,3,2,1,0:T(8,128)(2,1)S(1)}, bf16[2,2,2,32,1408]{4,3,2,1,0:T(8,128)(2,1)S(1)}, u32[]{:S(2)}, u32[]{:S(2)}) collective-permute-start(bf16[2,2,2,32,1408]{4,3,2,1,0:T(8,128)(2,1)S(1)} %maximum_select_fusion.3), channel_id=1, source_target_pairs={{0,2},{2,0},{4,6},{6,4},{8,10},{10,8},{12,14},{14,12},{16,18},{18,... | collective-permute-start | bytes 2162696 | tf_op jit(solution)/shard_map/ppermute | solution.py:20
  37.3 16.0 %collective-permute-start.6 = (bf16[2,2,2,32,1408]{4,3,0,1,2:T(8,128)(2,1)S(1)}, bf16[2,2,2,32,1408]{4,3,0,1,2:T(8,128)(2,1)S(1)}, u32[]{:S(2)}, u32[]{:S(2)}) collective-permute-start(bf16[2,2,2,32,1408]{4,3,0,1,2:T(8,128)(2,1)S(1)} %maximum_select_fusion.5), channel_id=1, source_target_pairs={{0,4},{2,6},{4,0},{6,2},{8,12},{10,14},{12,8},{14,10},{16,20},{18,... | collective-permute-start | bytes 2162696 | tf_op jit(solution)/shard_map/ppermute | solution.py:20
  56.1 2.7 %collective-permute-start.10 = (f32[512,512]{0,1:T(8,128)S(1)}, f32[512,512]{0,1:T(8,128)S(1)}, u32[]{:S(2)}, u32[]{:S(2)}) collective-permute-start(f32[512,512]{0,1:T(8,128)S(1)} %fusion.19), channel_id=1, source_target_pairs={{0,1},{1,0},{2,3},{3,2},{4,5},{5,4},{6,7},{7,6},{8,9},{9,8},{10,11... | collective-permute-start | bytes 3145736 | tf_op jit(solution)/shard_map/ppermute | solution.py:98
  60.9 28.3 %collective-permute-start.17 = (bf16[2,2,2,144,512]{4,3,0,2,1:T(8,128)(2,1)}, bf16[2,2,2,144,512]{4,3,0,2,1:T(8,128)(2,1)}, u32[]{:S(2)}, u32[]{:S(2)}) collective-permute-start(bf16[2,2,2,144,512]{4,3,0,2,1:T(8,128)(2,1)} %convolution_convert_fusion.1), channel_id=1, source_target_pairs={{0,8},{2,10},{4,12},{6,14},{8,0},{10,2},{12,4},{14,6},{16,24},{18,... | collective-permute-start | bytes 3538952 | tf_op jit(solution)/shard_map/ppermute | solution.py:20
  63.3 30.1 %collective-permute-start.14 = (bf16[2,2,2,144,512]{4,3,0,1,2:T(8,128)(2,1)}, bf16[2,2,2,144,512]{4,3,0,1,2:T(8,128)(2,1)}, u32[]{:S(2)}, u32[]{:S(2)}) collective-permute-start(bf16[2,2,2,144,512]{4,3,0,1,2:T(8,128)(2,1)} %convolution_convert_fusion.2), channel_id=1, source_target_pairs={{0,4},{2,6},{4,0},{6,2},{8,12},{10,14},{12,8},{14,10},{16,20},{18,... | collective-permute-start | bytes 3538952 | tf_op jit(solution)/shard_map/ppermute | solution.py:20
  66.4 30.7 %collective-permute-start.11 = (bf16[2,2,2,160,512]{4,3,2,1,0:T(8,128)(2,1)}, bf16[2,2,2,160,512]{4,3,2,1,0:T(8,128)(2,1)}, u32[]{:S(2)}, u32[]{:S(2)}) collective-permute-start(bf16[2,2,2,160,512]{4,3,2,1,0:T(8,128)(2,1)} %convolution_convert_fusion), channel_id=1, source_target_pairs={{0,2},{2,0},{4,6},{6,4},{8,10},{10,8},{12,14},{14,12},{16,18},{18,... | collective-permute-start | bytes 3932168 | tf_op jit(solution)/shard_map/ppermute | solution.py:20
  91.7 14.6 %collective-permute-start.18 = (bf16[2,2,144,512]{3,2,0,1:T(8,128)(2,1)S(1)}, bf16[2,2,144,512]{3,2,0,1:T(8,128)(2,1)S(1)}, u32[]{:S(2)}, u32[]{:S(2)}) collective-permute-start(bf16[2,2,144,512]{3,2,0,1:T(8,128)(2,1)S(1)} %fusion.29), channel_id=1, source_target_pairs={{0,4},{2,6},{4,0},{6,2},{8,12},{10,14},{12,8},{14,10},{16,20},{18,... | collective-permute-start | bytes 1769480 | tf_op jit(solution)/shard_map/ppermute | solution.py:20
  95.5 16.3 %collective-permute-start.15 = (bf16[2,2,144,512]{3,2,0,1:T(8,128)(2,1)S(1)}, bf16[2,2,144,512]{3,2,0,1:T(8,128)(2,1)S(1)}, u32[]{:S(2)}, u32[]{:S(2)}) collective-permute-start(bf16[2,2,144,512]{3,2,0,1:T(8,128)(2,1)S(1)} %fusion.28), channel_id=1, source_target_pairs={{0,2},{2,0},{4,6},{6,4},{8,10},{10,8},{12,14},{14,12},{16,18},{18,... | collective-permute-start | bytes 1769480 | tf_op jit(solution)/shard_map/ppermute | solution.py:20
  99.4 18.5 %collective-permute-start.12 = (bf16[2,2,160,512]{3,2,1,0:T(8,128)(2,1)S(1)}, bf16[2,2,160,512]{3,2,1,0:T(8,128)(2,1)S(1)}, u32[]{:S(2)}, u32[]{:S(2)}) collective-permute-start(bf16[2,2,160,512]{3,2,1,0:T(8,128)(2,1)S(1)} %fusion.27), channel_id=1, source_target_pairs={{0,8},{2,10},{4,12},{6,14},{8,0},{10,2},{12,4},{14,6},{16,24},{18,... | collective-permute-start | bytes 1966088 | tf_op jit(solution)/shard_map/ppermute | solution.py:20
  106.6 11.7 %collective-permute-start.19 = (bf16[2,144,512]{2,1,0:T(8,128)(2,1)S(1)}, bf16[2,144,512]{2,1,0:T(8,128)(2,1)S(1)}, u32[]{:S(2)}, u32[]{:S(2)}) collective-permute-start(bf16[2,144,512]{2,1,0:T(8,128)(2,1)S(1)} %fusion.39), channel_id=1, source_target_pairs={{0,2},{2,0},{4,6},{6,4},{8,10},{10,8},{12,14},{14,12},{16,18},{18,... | collective-permute-start | bytes 884744 | tf_op jit(solution)/shard_map/ppermute | solution.py:20
  112.1 9.1 %collective-permute-start.16 = (bf16[2,144,512]{2,1,0:T(8,128)(2,1)S(1)}, bf16[2,144,512]{2,1,0:T(8,128)(2,1)S(1)}, u32[]{:S(2)}, u32[]{:S(2)}) collective-permute-start(bf16[2,144,512]{2,1,0:T(8,128)(2,1)S(1)} %fusion.38), channel_id=1, source_target_pairs={{0,8},{2,10},{4,12},{6,14},{8,0},{10,2},{12,4},{14,6},{16,24},{18,... | collective-permute-start | bytes 884744 | tf_op jit(solution)/shard_map/ppermute | solution.py:20
  118.2 7.1 %collective-permute-start.13 = (bf16[2,160,512]{2,1,0:T(8,128)(2,1)S(1)}, bf16[2,160,512]{2,1,0:T(8,128)(2,1)S(1)}, u32[]{:S(2)}, u32[]{:S(2)}) collective-permute-start(bf16[2,160,512]{2,1,0:T(8,128)(2,1)S(1)} %fusion.37), channel_id=1, source_target_pairs={{0,4},{2,6},{4,0},{6,2},{8,12},{10,14},{12,8},{14,10},{16,20},{18,... | collective-permute-start | bytes 983048 | tf_op jit(solution)/shard_map/ppermute | solution.py:20
  127.9 17.5 %collective-permute-start.20 = (bf16[448,512]{1,0:T(8,128)(2,1)}, bf16[448,512]{1,0:T(8,128)(2,1)S(1)}, u32[]{:S(2)}, u32[]{:S(2)}) collective-permute-start(bf16[448,512]{1,0:T(8,128)(2,1)} %fusion.36), channel_id=1, source_target_pairs={{0,16},{2,18},{4,20},{6,22},{8,24},{10,26},{12,28},{14,30},{16,0},... | collective-permute-start | bytes 1376264 | tf_op jit(solution)/shard_map/ppermute | solution.py:20
  131.1 20.3 %copy-start.3 = (bf16[2,2,2,2,32,1408]{5,4,3,2,1,0:T(8,128)(2,1)S(1)}, bf16[2,2,2,2,32,1408]{5,4,3,2,1,0:T(8,128)(2,1)}, u32[]{:S(2)}) copy-start(bf16[2,2,2,2,32,1408]{5,4,3,2,1,0:T(8,128)(2,1)} %copy-done.2) | copy-start | bytes 4325380
  (6 other events, 11.6 us)
